TPU v7x, 32 devices: a whole 2x2x4 slice. The times are simulated.
32 devices in a mesh: fsdp: 8 (over z, y), context: 2 (over x), tensor: 2 (over core).
Axes of the slice: x: 2, y: 2, z: 4, core: 2. Of those that a mesh axis runs over, the one named last changes fastest.
Arguments:
- hidden_in: bfloat16 [8, 1024, 1024], P('fsdp', 'context', 'tensor')
- cotangent: bfloat16 [8, 1024, 1024], P('fsdp', 'context', 'tensor'), may hold values from -6 to 6
- segment: int32 [8, 1024], P('fsdp', 'context'), may hold values from 0 to 2, as said below
- position: int32 [8, 1024], P('fsdp', 'context'), may hold values from 0 to 1021, as said below
- w_query: bfloat16 [1024, 2048], P('fsdp', 'tensor'), may hold values from -0.1875 to 0.1875
- w_key: bfloat16 [1024, 1024], P('fsdp', 'tensor'), may hold values from -0.1875 to 0.1875
- w_value: bfloat16 [1024, 1024], P('fsdp', 'tensor'), may hold values from -0.1875 to 0.1875
- w_output: bfloat16 [2048, 1024], P('tensor', 'fsdp'), may hold values from -1 to 1
- w_gate: bfloat16 [1024, 3072], P('fsdp', 'tensor'), may hold values from -0.1875 to 0.1875
- w_up: bfloat16 [1024, 3072], P('fsdp', 'tensor'), may hold values from -0.1875 to 0.1875
- w_down: bfloat16 [3072, 1024], P('tensor', 'fsdp'), may hold values from -0.109375 to 0.109375
- attn_gain: bfloat16 [1024], P('fsdp'), may hold values from 0.099609375 to 1.8984375
- ffn_gain: bfloat16 [1024], P('fsdp'), may hold values from 0.099609375 to 1.8984375
- query_gain: bfloat16 [128], P('fsdp'), may hold values from 0.099609375 to 1.8984375
- key_gain: bfloat16 [128], P('fsdp'), may hold values from 0.099609375 to 1.8984375
Outputs:
- block_out: bfloat16 [8, 1024, 1024], P('fsdp', 'context', 'tensor')
- grad_input: float32 [8, 1024, 1024], P('fsdp', 'context', 'tensor')
- grad_w_query: float32 [1024, 2048], P('fsdp', 'tensor')
- grad_w_key: float32 [1024, 1024], P('fsdp', 'tensor')
- grad_w_value: float32 [1024, 1024], P('fsdp', 'tensor')
- grad_w_output: float32 [2048, 1024], P('tensor', 'fsdp')
- grad_w_gate: float32 [1024, 3072], P('fsdp', 'tensor')
- grad_w_up: float32 [1024, 3072], P('fsdp', 'tensor')
- grad_w_down: float32 [3072, 1024], P('tensor', 'fsdp')
- grad_attn_gain: float32 [1024], P('fsdp')
- grad_ffn_gain: float32 [1024], P('fsdp')
- grad_query_gain: float32 [128], P('fsdp')
- grad_key_gain: float32 [128], P('fsdp')
Inputs may be any that keep to these rules, and one draw needn't show every extreme that they name: `segment`: in every sequence the numbers never fall and all of 0, 1 and 2 occur; document 1 begins within the first 512 tokens (never at the first) and ends within the last 512 (never at the last); in one sequence of each draw it spans every token but the first and the last. `position`: 0 at each document's first token and rising by one along the document.
All inputs are finite; a program needn't handle non-finite values.
Results may differ from a plain program's by a relative error of at most 0.024.
Values may be sent and summed in bfloat16 or wider, within the bound.
No kernel may reach another device: no remote copies, remote signals or barrier semaphores. Data moves between devices by JAX's collectives and lax.ppermute only.
A program may use at most 192 MiB of HBM per device.

v0:
```python
import jax
import jax.numpy as jnp
from jax import lax
from jax.sharding import PartitionSpec as P

EPS = 1e-06
THETA = 1000000.0


def norm_stats(values):
    return lax.rsqrt(jnp.mean(values * values, axis=-1, keepdims=True) + EPS)


def norm_back(grad_out, normed, recip_root):
    return recip_root * (grad_out - normed * jnp.mean(grad_out * normed, axis=-1, keepdims=True))


def rotary_tables(position_row, head_size):
    half_size = head_size // 2
    freq_table = THETA ** (-jnp.arange(half_size, dtype=jnp.float32) * 2.0 / head_size)
    angle_table = position_row.astype(jnp.float32)[:, None] * freq_table[None, :]
    return (jnp.cos(angle_table)[:, None, :], jnp.sin(angle_table)[:, None, :])


def rotate(values, cosine_table, sine_table, turn_sign):
    half_size = values.shape[-1] // 2
    first_half = values[..., :half_size]
    second_half = values[..., half_size:]
    turned = turn_sign * sine_table
    return jnp.concatenate(
        [
            first_half * cosine_table - second_half * turned,
            second_half * cosine_table + first_half * turned,
        ],
        axis=-1,
    )


def shards(
    hidden_in,
    cotangent,
    segment,
    position,
    w_query,
    w_key,
    w_value,
    w_output,
    w_gate,
    w_up,
    w_down,
    attn_gain,
    ffn_gain,
    query_gain,
    key_gain,
):
    (
        wq_full,
        wk_full,
        wv_full,
        wo_full,
        wg_full,
        wu_full,
        wd_full,
        attn_full,
        ffn_full,
        qgain_full,
        kgain_full,
    ) = (
        lax.all_gather(w_query, "fsdp", axis=0, tiled=True),
        lax.all_gather(w_key, "fsdp", axis=0, tiled=True),
        lax.all_gather(w_value, "fsdp", axis=0, tiled=True),
        lax.all_gather(w_output, "fsdp", axis=1, tiled=True),
        lax.all_gather(w_gate, "fsdp", axis=0, tiled=True),
        lax.all_gather(w_up, "fsdp", axis=0, tiled=True),
        lax.all_gather(w_down, "fsdp", axis=1, tiled=True),
        lax.all_gather(attn_gain, "fsdp", axis=0, tiled=True),
        lax.all_gather(ffn_gain, "fsdp", axis=0, tiled=True),
        lax.all_gather(query_gain, "fsdp", axis=0, tiled=True),
        lax.all_gather(key_gain, "fsdp", axis=0, tiled=True),
    )
    rows_x, rows_dy = (
        lax.all_gather(hidden_in[0], "tensor", axis=1, tiled=True),
        lax.all_gather(cotangent[0], "tensor", axis=1, tiled=True),
    )
    tok_count = rows_x.shape[0]
    feat_part = hidden_in.shape[2]
    head_size = qgain_full.shape[0]
    q_heads = wq_full.shape[1] // head_size
    kv_heads = wk_full.shape[1] // head_size
    group_size = q_heads // kv_heads
    score_scale = head_size ** (-0.5)
    x_rows = rows_x.astype(jnp.float32)
    recip_one = norm_stats(x_rows)
    normed_one = x_rows * recip_one
    attn_gain32 = attn_full.astype(jnp.float32)
    attn_in = (normed_one * attn_gain32).astype(jnp.bfloat16)
    query_raw = jnp.dot(attn_in, wq_full, preferred_element_type=jnp.float32).reshape(
        tok_count, q_heads, head_size
    )
    key_raw = jnp.dot(attn_in, wk_full, preferred_element_type=jnp.float32).reshape(
        tok_count, kv_heads, head_size
    )
    value_raw = jnp.dot(attn_in, wv_full, preferred_element_type=jnp.float32)
    cosine_table, sine_table = rotary_tables(position[0], head_size)
    recip_query = norm_stats(query_raw)
    query_hat = query_raw * recip_query
    qgain32 = qgain_full.astype(jnp.float32)
    query_rot = rotate(query_hat * qgain32, cosine_table, sine_table, 1.0).astype(jnp.bfloat16)
    recip_key = norm_stats(key_raw)
    key_hat = key_raw * recip_key
    kgain32 = kgain_full.astype(jnp.float32)
    key_rot = rotate(key_hat * kgain32, cosine_table, sine_table, 1.0).astype(jnp.bfloat16)
    value_low = value_raw.astype(jnp.bfloat16).reshape(tok_count, kv_heads, head_size)
    key_all, value_all, segment_all = (
        lax.all_gather(key_rot, "context", axis=0, tiled=True),
        lax.all_gather(value_low, "context", axis=0, tiled=True),
        lax.all_gather(segment[0], "context", axis=0, tiled=True),
    )
    query_index = lax.axis_index("context") * tok_count + jnp.arange(tok_count, dtype=jnp.int32)
    key_index = jnp.arange(key_all.shape[0], dtype=jnp.int32)
    allowed = (segment[0][:, None] == segment_all[None, :]) & (
        key_index[None, :] <= query_index[:, None]
    )
    query_group = query_rot.reshape(tok_count, kv_heads, group_size, head_size)

    def scores_of():
        raw_scores = (
            jnp.einsum("pkgd,lkd->kgpl", query_group, key_all, preferred_element_type=jnp.float32)
            * score_scale
        )
        return jnp.where(allowed, raw_scores, -1e30)

    masked = scores_of()
    row_max = jnp.max(masked, axis=-1, keepdims=True)
    exp_terms = jnp.exp(masked - row_max)
    row_total = jnp.sum(exp_terms, axis=-1, keepdims=True)
    log_total = row_max + jnp.log(row_total)
    probs_fwd = (exp_terms / row_total).astype(jnp.bfloat16)
    attn_rows = jnp.einsum(
        "kgpl,lkd->pkgd", probs_fwd, value_all, preferred_element_type=jnp.float32
    )
    attn_low = attn_rows.reshape(tok_count, q_heads * head_size).astype(jnp.bfloat16)
    attn_sum = lax.psum(
        jnp.dot(attn_low, wo_full, preferred_element_type=jnp.float32).astype(jnp.bfloat16),
        "tensor",
    ).astype(jnp.float32)
    mid_rows = x_rows + attn_sum
    recip_two = norm_stats(mid_rows)
    normed_two = mid_rows * recip_two
    ffn_gain32 = ffn_full.astype(jnp.float32)
    ffn_in = (normed_two * ffn_gain32).astype(jnp.bfloat16)
    gate_pre = jnp.dot(ffn_in, wg_full, preferred_element_type=jnp.float32)
    up_pre = jnp.dot(ffn_in, wu_full, preferred_element_type=jnp.float32)
    gate_sig = jax.nn.sigmoid(gate_pre)
    gate_act = gate_pre * gate_sig
    hidden_low = (gate_act * up_pre).astype(jnp.bfloat16)
    ffn_rows = lax.psum_scatter(
        jnp.dot(hidden_low, wd_full, preferred_element_type=jnp.float32).astype(jnp.bfloat16),
        "tensor",
        scatter_dimension=1,
        tiled=True,
    ).astype(jnp.float32)
    feat_first = lax.axis_index("tensor") * feat_part
    mid_part = lax.dynamic_slice_in_dim(mid_rows, feat_first, feat_part, 1)
    block_out = (mid_part + ffn_rows).astype(jnp.bfloat16)[None]
    (
        wq_full,
        wk_full,
        wv_full,
        wo_full,
        wg_full,
        wu_full,
        wd_full,
        attn_full,
        ffn_full,
        qgain_full,
        kgain_full,
    ) = (
        lax.all_gather(w_query, "fsdp", axis=0, tiled=True),
        lax.all_gather(w_key, "fsdp", axis=0, tiled=True),
        lax.all_gather(w_value, "fsdp", axis=0, tiled=True),
        lax.all_gather(w_output, "fsdp", axis=1, tiled=True),
        lax.all_gather(w_gate, "fsdp", axis=0, tiled=True),
        lax.all_gather(w_up, "fsdp", axis=0, tiled=True),
        lax.all_gather(w_down, "fsdp", axis=1, tiled=True),
        lax.all_gather(attn_gain, "fsdp", axis=0, tiled=True),
        lax.all_gather(ffn_gain, "fsdp", axis=0, tiled=True),
        lax.all_gather(query_gain, "fsdp", axis=0, tiled=True),
        lax.all_gather(key_gain, "fsdp", axis=0, tiled=True),
    )
    grad_w_down = jnp.einsum("pf,pd->fd", hidden_low, rows_dy, preferred_element_type=jnp.float32)
    grad_hidden = jnp.einsum("pd,fd->pf", rows_dy, wd_full, preferred_element_type=jnp.float32)
    grad_gate = (grad_hidden * up_pre * gate_sig * (1.0 + gate_pre * (1.0 - gate_sig))).astype(
        jnp.bfloat16
    )
    grad_up_pre = (grad_hidden * gate_act).astype(jnp.bfloat16)
    grad_w_gate = jnp.einsum("pd,pf->df", ffn_in, grad_gate, preferred_element_type=jnp.float32)
    grad_w_up = jnp.einsum("pd,pf->df", ffn_in, grad_up_pre, preferred_element_type=jnp.float32)
    ffn_in_part = jnp.einsum(
        "pf,df->pd", grad_gate, wg_full, preferred_element_type=jnp.float32
    ) + jnp.einsum("pf,df->pd", grad_up_pre, wu_full, preferred_element_type=jnp.float32)
    grad_ffn_in = lax.psum(ffn_in_part.astype(jnp.bfloat16), "tensor").astype(jnp.float32)
    grad_ffn_gain = jnp.sum(grad_ffn_in * normed_two, axis=0)
    grad_mid = rows_dy.astype(jnp.float32) + norm_back(
        grad_ffn_in * ffn_gain32, normed_two, recip_two
    )
    grad_mid_low = grad_mid.astype(jnp.bfloat16)
    grad_w_output = jnp.einsum(
        "pf,pd->fd", attn_low, grad_mid_low, preferred_element_type=jnp.float32
    )
    grad_attn = jnp.einsum("pd,fd->pf", grad_mid_low, wo_full, preferred_element_type=jnp.float32)
    grad_attn = grad_attn.astype(jnp.bfloat16).reshape(tok_count, kv_heads, group_size, head_size)
    soft_probs = jnp.exp(scores_of() - log_total)
    grad_probs = jnp.einsum(
        "pkgd,lkd->kgpl", grad_attn, value_all, preferred_element_type=jnp.float32
    )
    row_delta = jnp.sum(soft_probs * grad_probs, axis=-1, keepdims=True)
    grad_scores = (soft_probs * (grad_probs - row_delta)).astype(jnp.bfloat16)
    probs_low = soft_probs.astype(jnp.bfloat16)
    grad_query = (
        jnp.einsum("kgpl,lkd->pkgd", grad_scores, key_all, preferred_element_type=jnp.float32)
        * score_scale
    )
    grad_query = grad_query.reshape(tok_count, q_heads, head_size)
    grad_key_rows = (
        jnp.einsum("kgpl,pkgd->lkd", grad_scores, query_group, preferred_element_type=jnp.float32)
        * score_scale
    )
    grad_value_rows = jnp.einsum(
        "kgpl,pkgd->lkd", probs_low, grad_attn, preferred_element_type=jnp.float32
    )
    key_value_grads = lax.psum_scatter(
        jnp.concatenate(
            [
                grad_key_rows.reshape(tok_count * lax.axis_size("context"), -1),
                grad_value_rows.reshape(tok_count * lax.axis_size("context"), -1),
            ],
            axis=1,
        ).astype(jnp.bfloat16),
        "context",
        scatter_dimension=0,
        tiled=True,
    ).astype(jnp.float32)
    kv_width = kv_heads * head_size
    grad_key = key_value_grads[:, :kv_width].reshape(tok_count, kv_heads, head_size)
    grad_value_low = key_value_grads[:, kv_width:].astype(jnp.bfloat16)
    unrot_query = rotate(grad_query, cosine_table, sine_table, -1.0)
    grad_query_gain = jnp.sum(unrot_query * query_hat, axis=(0, 1))
    grad_query_raw = (
        norm_back(unrot_query * qgain32, query_hat, recip_query)
        .astype(jnp.bfloat16)
        .reshape(tok_count, q_heads * head_size)
    )
    unrot_key = rotate(grad_key, cosine_table, sine_table, -1.0)
    grad_key_gain = jnp.sum(unrot_key * key_hat, axis=(0, 1))
    grad_key_raw = (
        norm_back(unrot_key * kgain32, key_hat, recip_key)
        .astype(jnp.bfloat16)
        .reshape(tok_count, kv_width)
    )
    grad_w_query = jnp.einsum(
        "pd,pf->df", attn_in, grad_query_raw, preferred_element_type=jnp.float32
    )
    grad_w_key = jnp.einsum("pd,pf->df", attn_in, grad_key_raw, preferred_element_type=jnp.float32)
    grad_w_value = jnp.einsum(
        "pd,pf->df", attn_in, grad_value_low, preferred_element_type=jnp.float32
    )
    attn_in_part = (
        jnp.einsum("pf,df->pd", grad_query_raw, wq_full, preferred_element_type=jnp.float32)
        + jnp.einsum("pf,df->pd", grad_key_raw, wk_full, preferred_element_type=jnp.float32)
        + jnp.einsum("pf,df->pd", grad_value_low, wv_full, preferred_element_type=jnp.float32)
    )
    grad_attn_in, grad_query_gain, grad_key_gain = (
        lax.psum(attn_in_part.astype(jnp.bfloat16), "tensor").astype(jnp.float32),
        lax.psum(grad_query_gain.astype(jnp.bfloat16), "tensor").astype(jnp.float32),
        lax.psum(grad_key_gain.astype(jnp.bfloat16), "tensor").astype(jnp.float32),
    )
    grad_attn_gain = jnp.sum(grad_attn_in * normed_one, axis=0)
    grad_input = grad_mid + norm_back(
        grad_attn_in * attn_full.astype(jnp.float32), normed_one, recip_one
    )
    grad_input_part = lax.dynamic_slice_in_dim(grad_input, feat_first, feat_part, 1)[None]
    owned = (
        lax.psum_scatter(
            grad_w_query.astype(jnp.bfloat16), "fsdp", scatter_dimension=0, tiled=True
        ).astype(jnp.float32),
        lax.psum_scatter(
            grad_w_key.astype(jnp.bfloat16), "fsdp", scatter_dimension=0, tiled=True
        ).astype(jnp.float32),
        lax.psum_scatter(
            grad_w_value.astype(jnp.bfloat16), "fsdp", scatter_dimension=0, tiled=True
        ).astype(jnp.float32),
        lax.psum_scatter(
            grad_w_output.astype(jnp.bfloat16), "fsdp", scatter_dimension=1, tiled=True
        ).astype(jnp.float32),
        lax.psum_scatter(
            grad_w_gate.astype(jnp.bfloat16), "fsdp", scatter_dimension=0, tiled=True
        ).astype(jnp.float32),
        lax.psum_scatter(
            grad_w_up.astype(jnp.bfloat16), "fsdp", scatter_dimension=0, tiled=True
        ).astype(jnp.float32),
        lax.psum_scatter(
            grad_w_down.astype(jnp.bfloat16), "fsdp", scatter_dimension=1, tiled=True
        ).astype(jnp.float32),
        lax.psum_scatter(
            grad_attn_gain.astype(jnp.bfloat16), "fsdp", scatter_dimension=0, tiled=True
        ).astype(jnp.float32),
        lax.psum_scatter(
            grad_ffn_gain.astype(jnp.bfloat16), "fsdp", scatter_dimension=0, tiled=True
        ).astype(jnp.float32),
        lax.psum_scatter(
            grad_query_gain.astype(jnp.bfloat16), "fsdp", scatter_dimension=0, tiled=True
        ).astype(jnp.float32),
        lax.psum_scatter(
            grad_key_gain.astype(jnp.bfloat16), "fsdp", scatter_dimension=0, tiled=True
        ).astype(jnp.float32),
    )
    owned = (
        lax.psum(owned[0].astype(jnp.bfloat16), "context").astype(jnp.float32),
        lax.psum(owned[1].astype(jnp.bfloat16), "context").astype(jnp.float32),
        lax.psum(owned[2].astype(jnp.bfloat16), "context").astype(jnp.float32),
        lax.psum(owned[3].astype(jnp.bfloat16), "context").astype(jnp.float32),
        lax.psum(owned[4].astype(jnp.bfloat16), "context").astype(jnp.float32),
        lax.psum(owned[5].astype(jnp.bfloat16), "context").astype(jnp.float32),
        lax.psum(owned[6].astype(jnp.bfloat16), "context").astype(jnp.float32),
        lax.psum(owned[7].astype(jnp.bfloat16), "context").astype(jnp.float32),
        lax.psum(owned[8].astype(jnp.bfloat16), "context").astype(jnp.float32),
        lax.psum(owned[9].astype(jnp.bfloat16), "context").astype(jnp.float32),
        lax.psum(owned[10].astype(jnp.bfloat16), "context").astype(jnp.float32),
    )
    return (
        block_out,
        grad_input_part,
        owned[0],
        owned[1],
        owned[2],
        owned[3],
        owned[4],
        owned[5],
        owned[6],
        owned[7],
        owned[8],
        owned[9],
        owned[10],
    )


def solution(mesh):
    in_specs = (
        P("fsdp", "context", "tensor"),
        P("fsdp", "context", "tensor"),
        P("fsdp", "context"),
        P("fsdp", "context"),
        P("fsdp", "tensor"),
        P("fsdp", "tensor"),
        P("fsdp", "tensor"),
        P("tensor", "fsdp"),
        P("fsdp", "tensor"),
        P("fsdp", "tensor"),
        P("tensor", "fsdp"),
        P("fsdp"),
        P("fsdp"),
        P("fsdp"),
        P("fsdp"),
    )
    out_specs = (
        P("fsdp", "context", "tensor"),
        P("fsdp", "context", "tensor"),
        P("fsdp", "tensor"),
        P("fsdp", "tensor"),
        P("fsdp", "tensor"),
        P("tensor", "fsdp"),
        P("fsdp", "tensor"),
        P("fsdp", "tensor"),
        P("tensor", "fsdp"),
        P("fsdp"),
        P("fsdp"),
        P("fsdp"),
        P("fsdp"),
    )
    return jax.shard_map(shards, mesh=mesh, in_specs=in_specs, out_specs=out_specs, check_vma=False)
```

profile of v0, /device:TPU:0, one launch (start us, length us, event | category | flops | bytes accessed | tf_op | source)
XLA Modules:
  0.0 1220.7 jit_solution(10290824358312127259)
XLA Ops:
  13.7 23.2 %all-reduce.7 = (bf16[128]{0:T(256)(128)(2,1)S(1)}, bf16[128]{0:T(256)(128)(2,1)S(1)}) all-reduce(bf16[128]{0:T(256)(128)(2,1)S(1)} %dynamic-update-slice, bf16[128]{0:T(256)(128)(2,1)S(1)} %dynamic-update-slice.1), channel_id=1, replica_groups=mesh['fsdp'=8,'context'=2,'tensor'=2] {'fsdp'}, use_global_device_ids=true, to_apply=%add | all-reduce | flops 256 | bytes 1024
  37.6 16.5 %all-gather.3 = bf16[8,1,128]{2,1,0:T(2,128)(2,1)S(1)} all-gather(bf16[1,1,128]{2,1,0:T(2,128)(2,1)} %bitcast.253), channel_id=1, replica_groups=mesh['fsdp'=8,'context'=2,'tensor'=2] {'fsdp'}, dimensions={0}, use_global_device_ids=true | all-gather | bytes 2304 | tf_op jit(solution)/shard_map/all_gather | solution.py:76
  70.4 35.5 %all-gather.17.cloned.1.call-done = bf16[1024,512]{1,0:T(8,128)(2,1)} async-done(((bf16[128,512]{1,0:T(8,128)(2,1)}), bf16[1024,512]{1,0:T(8,128)(2,1)}) %all-gather.17.cloned.1.call-update) | async-done | bytes 1048592 | tf_op jit(solution)/shard_map/all_gather | solution.py:71
  115.5 40.5 %all-gather.25.cloned.1.call-done = bf16[1024,1024]{1,0:T(8,128)(2,1)} async-done(((bf16[128,1024]{1,0:T(8,128)(2,1)}), bf16[1024,1024]{1,0:T(8,128)(2,1)}) %all-gather.25.cloned.1.call-update) | async-done | bytes 2097168 | tf_op jit(solution)/shard_map/all_gather | solution.py:69
  164.3 13.4 %all-gather.23.cloned.1.call-done = bf16[1024,4,128]{2,0,1:T(8,128)(2,1)} async-done(((bf16[512,4,128]{2,0,1:T(8,128)(2,1)}), bf16[1024,4,128]{2,0,1:T(8,128)(2,1)}) %all-gather.23.cloned.1.call-update) | async-done | bytes 1048592 | tf_op jit(solution)/shard_map/all_gather | solution.py:115
  210.3 43.9 %all-gather.27.cloned.1.call-done = bf16[1024,1024]{1,0:T(8,128)(2,1)} async-done(((bf16[1024,128]{1,0:T(8,128)(2,1)}), bf16[1024,1024]{1,0:T(8,128)(2,1)}) %all-gather.27.cloned.1.call-update) | async-done | bytes 2097168 | tf_op jit(solution)/shard_map/all_gather | solution.py:72
  260.8 18.0 %all-gather.4 = bf16[8,1,128]{2,1,0:T(2,128)(2,1)S(1)} all-gather(bf16[1,1,128]{2,1,0:T(2,128)(2,1)S(1)} %bitcast.254), channel_id=1, replica_groups=mesh['fsdp'=8,'context'=2,'tensor'=2] {'fsdp'}, dimensions={0}, use_global_device_ids=true | all-gather | bytes 2304 | tf_op jit(solution)/shard_map/all_gather | solution.py:77
  281.0 59.1 %all-gather.31.cloned.1.call-done = bf16[1024,1536]{1,0:T(8,128)(2,1)} async-done(((bf16[128,1536]{1,0:T(8,128)(2,1)}), bf16[1024,1536]{1,0:T(8,128)(2,1)}) %all-gather.31.cloned.1.call-update) | async-done | bytes 3145744 | tf_op jit(solution)/shard_map/all_gather | solution.py:74
  345.6 55.9 %all-gather.29.cloned.1.call-done = bf16[1024,1536]{1,0:T(8,128)(2,1)} async-done(((bf16[128,1536]{1,0:T(8,128)(2,1)}), bf16[1024,1536]{1,0:T(8,128)(2,1)}) %all-gather.29.cloned.1.call-update) | async-done | bytes 3145744 | tf_op jit(solution)/shard_map/all_gather | solution.py:73
  410.8 66.4 %all-gather.33.cloned.1.call-done = bf16[1536,1024]{1,0:T(8,128)(2,1)} async-done(((bf16[1536,128]{1,0:T(8,128)(2,1)}), bf16[1536,1024]{1,0:T(8,128)(2,1)}) %all-gather.33.cloned.1.call-update) | async-done | bytes 3145744 | tf_op jit(solution)/shard_map/all_gather | solution.py:75
  491.3 17.9 %all-reduce.18.cloned.1.call-done = bf16[512,1024]{1,0:T(8,128)(2,1)} async-done(((bf16[512,1024]{1,0:T(8,128)(2,1)}), bf16[512,1024]{1,0:T(8,128)(2,1)}) %all-reduce.18.cloned.1.call-update) | async-done | bytes 1048592 | tf_op jit(solution)/shard_map/psum | solution.py:202
  519.8 9.8 bitcast_convert_fusion
  529.7 16.1 %fusion = (f32[4,2,512]{2,1,0:T(2,128)}, f32[4,1024,512,2]{2,1,3,0:T(8,128)}) fusion(f32[4,2,512,1024]{2,3,1,0:T(8,128)} %get-tuple-element.71, f32[4,2,512]{2,1,0:T(2,128)} %bitcast.235, bf16[512,4,2,128]{0,3,2,1:T(8,128)(2,1)} %bitcast.215, bf16[1024,4,128]{0,2,1:T(8,128)(2,1)} %all-gather.19.cloned.1.call-done), kind=kOutput, calls=%fused_computation.2 | convolution fusion | flops 1086320640 | bytes 35684352 | tf_op jit(solution)/shard_map/pkgd,lkd->kgpl/dot_general | solution.py:214
  545.8 11.0 fusion.2
  646.3 22.9 %reduce-scatter.28.cloned.1.call-done = bf16[128,1024]{1,0:T(8,128)(2,1)} async-done(((bf16[1024,1024]{1,0:T(8,128)(2,1)}), bf16[128,1024]{1,0:T(8,128)(2,1)}) %reduce-scatter.28.cloned.1.call-update) | async-done | bytes 262160
  671.0 75.6 %reduce-scatter.30.cloned.1.call-done = bf16[128,1536]{1,0:T(8,128)(2,1)} async-done(((bf16[1024,1536]{1,0:T(8,128)(2,1)}), bf16[128,1536]{1,0:T(8,128)(2,1)}) %reduce-scatter.30.cloned.1.call-update) | async-done | bytes 393232
  748.6 68.7 %reduce-scatter.18.cloned.1.call-done = bf16[128,1024]{1,0:T(8,128)(2,1)} async-done(((bf16[1024,1024]{1,0:T(8,128)(2,1)}), bf16[128,1024]{1,0:T(8,128)(2,1)}) %reduce-scatter.18.cloned.1.call-update) | async-done | bytes 262160 | tf_op jit(solution)/shard_map/reduce_scatter | solution.py:284
  817.3 77.2 %reduce-scatter.26.cloned.1.call-done = bf16[128,1536]{1,0:T(8,128)(2,1)} async-done(((bf16[1024,1536]{1,0:T(8,128)(2,1)}), bf16[128,1536]{1,0:T(8,128)(2,1)}) %reduce-scatter.26.cloned.1.call-update) | async-done | bytes 393232 | tf_op jit(solution)/shard_map/reduce_scatter | solution.py:299
  894.5 77.7 %reduce-scatter.24.cloned.1.call-done = bf16[128,1536]{1,0:T(8,128)(2,1)} async-done(((bf16[1024,1536]{1,0:T(8,128)(2,1)}), bf16[128,1536]{1,0:T(8,128)(2,1)}) %reduce-scatter.24.cloned.1.call-update) | async-done | bytes 393232 | tf_op jit(solution)/shard_map/reduce_scatter | solution.py:296
  972.2 66.3 %reduce-scatter.20.cloned.1.call-done = bf16[128,512]{1,0:T(8,128)(2,1)} async-done(((bf16[1024,512]{1,0:T(8,128)(2,1)}), bf16[128,512]{1,0:T(8,128)(2,1)}) %reduce-scatter.20.cloned.1.call-update) | async-done | bytes 131088 | tf_op jit(solution)/shard_map/reduce_scatter | solution.py:287
  1038.4 65.8 %reduce-scatter.22.cloned.1.call-done = bf16[128,512]{1,0:T(8,128)(2,1)} async-done(((bf16[1024,512]{1,0:T(8,128)(2,1)}), bf16[128,512]{1,0:T(8,128)(2,1)}) %reduce-scatter.22.cloned.1.call-update) | async-done | bytes 131088 | tf_op jit(solution)/shard_map/reduce_scatter | solution.py:290
  1105.6 19.7 %all-reduce.20.cloned.1.call-done = bf16[512,1024]{1,0:T(8,128)(2,1)} async-done(((bf16[512,1024]{1,0:T(8,128)(2,1)}), bf16[512,1024]{1,0:T(8,128)(2,1)}) %all-reduce.20.cloned.1.call-update) | async-done | bytes 1048592 | tf_op jit(solution)/shard_map/psum | solution.py:274
  1129.2 22.0 %all-reduce.6 = (bf16[1024]{0:T(1024)(128)(2,1)S(1)}, bf16[1024]{0:T(1024)(128)(2,1)S(1)}, bf16[128]{0:T(256)(128)(2,1)S(1)}, bf16[128]{0:T(256)(128)(2,1)S(1)}) all-reduce(bf16[1024]{0:T(1024)(128)(2,1)S(1)} %get-tuple-element.15, ...), channel_id=14, replica_groups=mesh['fsdp'=8,'context'=2,'tensor'=2] {'fsdp'}, use_global_device_ids=true, to_apply=%region_31.32.clone | all-reduce | flops 2304 | bytes 9216
  1166.1 37.4 %all-reduce.22.cloned.1.call-done = (bf16[128,1024]{1,0:T(8,128)(2,1)}, bf16[128,512]{1,0:T(8,128)(2,1)}, bf16[128,512]{1,0:T(8,128)(2,1)}, bf16[1024,128]{1,0:T...) async-done(((bf16[128,1024]{1,0:T(8,128)(2,1)}, bf16[128,512]{1,0:T(8,128)(2,1)}, bf16[128,512]{1,0:T(8,128)(2,1)}, ...) | async-done | bytes 1966096 | tf_op jit(solution)/shard_map/psum | solution.py:319
  (289 shorter events, 242.5 us)
Async XLA Ops:
  7.2 48.8 %all-gather.35.cloned.1.call-start = ((), (), s32[]{:S(2)}) async-start(), calls=%async_computation.28 | async-start | bytes 1572864 | tf_op jit(solution)/shard_map/all_gather | solution.py:82
  7.9 56.9 %all-gather.21.cloned.1.call-start = ((), (), s32[]{:S(2)}) async-start(), calls=%async_computation.11 | async-start | bytes 1179648 | tf_op jit(solution)/shard_map/all_gather | solution.py:70
  8.7 97.3 %all-gather.17.cloned.1.call-start = ((), (), s32[]{:S(2)}) async-start(), calls=%async_computation.9 | async-start | bytes 1179648 | tf_op jit(solution)/shard_map/all_gather | solution.py:71
  9.4 146.6 %all-gather.25.cloned.1.call-start = ((), (), s32[]{:S(2)}) async-start(), calls=%async_computation.13 | async-start | bytes 2359296 | tf_op jit(solution)/shard_map/all_gather | solution.py:69
  10.0 167.8 %all-gather.23.cloned.1.call-start = ((), (), s32[]{:S(2)}) async-start(), calls=%async_computation.12 | async-start | bytes 1572864 | tf_op jit(solution)/shard_map/all_gather | solution.py:115
  70.3 130.7 %all-gather.19.cloned.1.call-start = ((), (), s32[]{:S(2)}) async-start(), calls=%async_computation.10 | async-start | bytes 1572864 | tf_op jit(solution)/shard_map/all_gather | solution.py:116
  108.8 145.4 %all-gather.27.cloned.1.call-start = ((), (), s32[]{:S(2)}) async-start(), calls=%async_computation.14 | async-start | bytes 2359296 | tf_op jit(solution)/shard_map/all_gather | solution.py:72
  109.6 169.2 %all-reduce.16.cloned.1.call-start = ((), (), s32[]{:S(2)}) async-start(), calls=%async_computation.15 | async-start | bytes 2097152 | tf_op jit(solution)/shard_map/psum | solution.py:143
  258.1 82.0 %all-gather.31.cloned.1.call-start = ((), (), s32[]{:S(2)}) async-start(), calls=%async_computation.17 | async-start | bytes 3538944 | tf_op jit(solution)/shard_map/all_gather | solution.py:74
  258.8 142.7 %all-gather.29.cloned.1.call-start = ((), (), s32[]{:S(2)}) async-start(), calls=%async_computation.16 | async-start | bytes 3538944 | tf_op jit(solution)/shard_map/all_gather | solution.py:73
  259.4 151.4 %all-gather.37.cloned.1.call-start = ((), (), s32[]{:S(2)}) async-start(), calls=%async_computation.29 | async-start | bytes 1572864 | tf_op jit(solution)/shard_map/all_gather | solution.py:83
  260.2 217.0 %all-gather.33.cloned.1.call-start = ((), (), s32[]{:S(2)}) async-start(), calls=%async_computation.18 | async-start | bytes 3538944 | tf_op jit(solution)/shard_map/all_gather | solution.py:75
  260.7 248.5 %all-reduce.18.cloned.1.call-start = ((), (), s32[]{:S(2)}) async-start(), calls=%async_computation.20 | async-start | bytes 2097152 | tf_op jit(solution)/shard_map/psum | solution.py:202
  491.2 130.0 %reduce-scatter.16.cloned.1.call-start = ((), (), s32[]{:S(2)}) async-start(), calls=%async_computation.21 | async-start | bytes 3145728 | tf_op jit(solution)/shard_map/reduce_scatter | solution.py:232
  564.5 104.7 %reduce-scatter.28.cloned.1.call-start = ((), (), s32[]{:S(2)}) async-start(), calls=%async_computation.30 | async-start | bytes 2359296
  573.8 172.8 %reduce-scatter.30.cloned.1.call-start = ((), (), s32[]{:S(2)}) async-start(), calls=%async_computation.31 | async-start | bytes 3538944
  584.7 232.6 %reduce-scatter.18.cloned.1.call-start = ((), (), s32[]{:S(2)}) async-start(), calls=%async_computation.23 | async-start | bytes 2359296 | tf_op jit(solution)/shard_map/reduce_scatter | solution.py:284
  609.3 285.2 %reduce-scatter.26.cloned.1.call-start = ((), (), s32[]{:S(2)}) async-start(), calls=%async_computation.27 | async-start | bytes 3538944 | tf_op jit(solution)/shard_map/reduce_scatter | solution.py:299
  615.4 356.8 %reduce-scatter.24.cloned.1.call-start = ((), (), s32[]{:S(2)}) async-start(), calls=%async_computation.26 | async-start | bytes 3538944 | tf_op jit(solution)/shard_map/reduce_scatter | solution.py:296
  620.6 417.8 %reduce-scatter.20.cloned.1.call-start = ((), (), s32[]{:S(2)}) async-start(), calls=%async_computation.24 | async-start | bytes 1179648 | tf_op jit(solution)/shard_map/reduce_scatter | solution.py:287
  632.8 471.4 %reduce-scatter.22.cloned.1.call-start = ((), (), s32[]{:S(2)}) async-start(), calls=%async_computation.25 | async-start | bytes 1179648 | tf_op jit(solution)/shard_map/reduce_scatter | solution.py:290
  634.8 490.5 %all-reduce.20.cloned.1.call-start = ((), (), s32[]{:S(2)}) async-start(), calls=%async_computation.22 | async-start | bytes 2097152 | tf_op jit(solution)/shard_map/psum | solution.py:274
  641.5 509.9 %reduce-scatter.14.cloned.1.call-start = ((), (), s32[]{:S(2)}) async-start(), calls=%async_computation.19 | async-start | bytes 1572864 | tf_op jit(solution)/shard_map/reduce_scatter | solution.py:157
  646.3 557.3 %all-reduce.22.cloned.1.call-start = ((), (), s32[]{:S(2)}) async-start(), calls=%async_computation.32 | async-start | bytes 3932160 | tf_op jit(solution)/shard_map/psum | solution.py:319
  (61 other events, 875.5 us)
Sparse Core Ops, SparseCore 0:
  9.6 11.7 all-gather.34
  23.4 41.3 all-gather.20
  67.0 38.8 all-gather.16
  107.9 48.0 all-gather.24
  157.9 19.7 all-gather.22
  179.7 21.2 all-gather.18
  203.1 51.0 all-gather.26
  258.2 17.7 all-reduce.15
  278.5 61.6 all-gather.30
  342.4 59.0 all-gather.28
  403.1 7.6 all-gather.36
  412.9 64.2 all-gather.32
  491.4 17.7 all-reduce.17
  564.6 32.9 reduce-scatter.15
  601.4 67.7 reduce-scatter.27
  673.1 73.5 reduce-scatter.29
  750.5 66.7 reduce-scatter.17
  821.1 73.3 reduce-scatter.25
  898.5 73.6 reduce-scatter.23
  975.8 62.5 reduce-scatter.19
  1041.8 62.3 reduce-scatter.21
  1106.7 18.6 all-reduce.19
  1128.1 9.7 reduce-scatter.13
  1141.2 62.2 all-reduce.21
where the time goes:
time: 1230 us; the launch traced here: 1220 us
  waiting for transfers between devices  867 us (70%)
  matrix products  128 us (10%)
  blocking collectives  91.7 us (7%)
  other arithmetic  69.3 us (6%)
  local copies, waits for them, and re-layouts  46 us (4%)
  between operations  17.5 us (1%)
    unnamed x26, waiting for transfers between devices  104 us
    reduce_scatter x1, waiting for transfers between devices, shards(): lax.psum_scatter(grad_w_gate.astype(jnp.bfloat16), 'fsdp', scatter_dimens...  77.7 us
    reduce_scatter x1, waiting for transfers between devices, shards(): lax.psum_scatter(grad_w_up.astype(jnp.bfloat16), 'fsdp', scatter_dimensio...  77.2 us
    reduce_scatter x1, waiting for transfers between devices, shards(): lax.psum_scatter(grad_w_query.astype(jnp.bfloat16), 'fsdp', scatter_dimen...  68.7 us
    all_gather x1, waiting for transfers between devices, shards(): lax.all_gather(w_down, 'fsdp', axis=1, tiled=True)  66.4 us
    reduce_scatter x1, waiting for transfers between devices, shards(): lax.psum_scatter(grad_w_key.astype(jnp.bfloat16), 'fsdp', scatter_dimensi...  66.3 us
    reduce_scatter x1, waiting for transfers between devices, shards(): lax.psum_scatter(grad_w_value.astype(jnp.bfloat16), 'fsdp', scatter_dimen...  65.8 us
    all_gather x1, waiting for transfers between devices, shards(): lax.all_gather(w_up, 'fsdp', axis=0, tiled=True)  59.1 us
  transfers between devices with their start and end apart: 24, of which 20 were waited for; matrix products, arithmetic and copies ran while one was open for 12% of the time, Pallas kernels for 0%

commit v1 on v0

--- a/solution.py
+++ b/solution.py
@@ -1,6 +1,8 @@
 import jax
 import jax.numpy as jnp
 from jax import lax
+from jax.experimental import pallas as pl
+from jax.experimental.pallas import tpu as pltpu
 from jax.sharding import PartitionSpec as P
 
 EPS = 1e-06
@@ -36,7 +38,7 @@
     )
 
 
-def shards(
+def plain_shards(
     hidden_in,
     cotangent,
     segment,
@@ -345,6 +347,779 @@
     )
 
 
+def fence(*values):
+    return lax.optimization_barrier(values)
+
+
+def after(value, *earlier):
+    return lax.optimization_barrier((value,) + earlier)[0]
+
+
+def swap(values, axis_name):
+    return lax.ppermute(values, axis_name, [(0, 1), (1, 0)])
+
+
+def pick(index, zero_item, one_item):
+    return jnp.where(index == 0, zero_item, one_item)
+
+
+def pair_join(index, own, other, axis):
+    return jnp.concatenate([pick(index, own, other), pick(index, other, own)], axis=axis)
+
+
+def half_of(values, index, axis):
+    half = values.shape[axis] // 2
+    return lax.dynamic_slice_in_dim(values, index * half, half, axis)
+
+
+def ring_pairs(fsdp_size):
+    columns = fsdp_size // 2
+    flip = [(i, i ^ 1) for i in range(fsdp_size)]
+
+    def turn(step):
+        return [
+            (z * 2 + y, ((z + step) % columns) * 2 + y) for z in range(columns) for y in range(2)
+        ]
+
+    return columns, flip, turn
+
+
+def copy_call(copies_of, scalars, operands, shapes, copy_count, spaces):
+    operand_count, result_count = len(operands), len(shapes)
+
+    def kernel(scalar_ref, *refs):
+        sources = refs[:operand_count]
+        targets = refs[operand_count : operand_count + result_count]
+        sems = refs[operand_count + result_count]
+        copies = [
+            pltpu.make_async_copy(source, target, sems.at[i])
+            for i, (source, target) in enumerate(copies_of(scalar_ref, sources, targets))
+        ]
+        for copy in copies:
+            copy.start()
+        for copy in copies:
+            copy.wait()
+
+    moved = sum(2 * shape.size * shape.dtype.itemsize for shape in shapes)
+    return pl.pallas_call(
+        kernel,
+        out_shape=shapes,
+        in_specs=[pl.BlockSpec(memory_space=pltpu.SMEM)]
+        + [pl.BlockSpec(memory_space=spaces[0])] * operand_count,
+        out_specs=[pl.BlockSpec(memory_space=spaces[1])] * result_count,
+        scratch_shapes=[pltpu.SemaphoreType.DMA((copy_count,))],
+        compiler_params=pltpu.CompilerParams(vmem_limit_bytes=32 * 1024 * 1024),
+        cost_estimate=pl.CostEstimate(flops=0, bytes_accessed=moved, transcendentals=0),
+    )(jnp.stack(scalars).astype(jnp.int32), *operands)
+
+
+def pack_call(x_index, kv_heads, head_size, w_query, w_key, w_value, gain_rows):
+    rows, q_columns = w_query.shape
+    group_width = q_columns // (2 * kv_heads)
+    wide = group_width + 2 * head_size
+
+    def kernel(x_ref, query_ref, key_ref, value_ref, gain_ref, out_ref):
+        x = x_ref[0]
+        for g in range(kv_heads):
+            first = g * wide
+            for ref, size in ((query_ref, group_width), (key_ref, head_size), (value_ref, head_size)):
+                start = pl.multiple_of((x * kv_heads + g) * size, size)
+                out_ref[:rows, first : first + size] = ref[:, pl.ds(start, size)]
+                first += size
+        out_ref[rows:, :] = gain_ref[...]
+
+    return pl.pallas_call(
+        kernel,
+        out_shape=jax.ShapeDtypeStruct(
+            (rows + gain_rows.shape[0], kv_heads * wide), w_query.dtype
+        ),
+        in_specs=[pl.BlockSpec(memory_space=pltpu.SMEM)]
+        + [pl.BlockSpec(memory_space=pltpu.VMEM)] * 4,
+        out_specs=pl.BlockSpec(memory_space=pltpu.VMEM),
+    )(x_index.astype(jnp.int32)[None], w_query, w_key, w_value, gain_rows)
+
+
+def turn_pieces(blob):
+    columns, _, turn = ring_pairs(lax.axis_size("fsdp"))
+    return [blob] + [lax.ppermute(blob, "fsdp", turn(step)) for step in range(1, columns)]
+
+
+def flip_pieces(values):
+    return lax.ppermute(values, "fsdp", ring_pairs(lax.axis_size("fsdp"))[1])
+
+
+def stack_pieces(first, rest):
+    pieces = [first] + list(rest)
+    shape = (len(pieces),) + pieces[0].shape
+    return copy_call(
+        lambda at, own, out: [(piece, out[0].at[i]) for i, piece in enumerate(own)],
+        [jnp.int32(0)],
+        pieces,
+        [jax.ShapeDtypeStruct(shape, pieces[0].dtype)],
+        len(pieces),
+        (pltpu.VMEM, pl.ANY),
+    )[0]
+
+
+def place_rows(near, far):
+    fsdp_size = lax.axis_size("fsdp")
+    columns = fsdp_size // 2
+    place = lax.axis_index("fsdp")
+    column, side = place // 2, place % 2
+    sources = [(column - step + columns) % columns for step in range(columns)]
+    near_at = [source * 2 + side for source in sources]
+    far_at = [source * 2 + 1 - side for source in sources]
+    operands = list(near) + list(far)
+
+    def copies_of(at, own, out):
+        copies, slot = [], 0
+        for ref in own:
+            if len(ref.shape) == 2:
+                copies.append((ref, out[0].at[at[slot]]))
+                slot += 1
+                continue
+            for i in range(ref.shape[0]):
+                copies.append((ref.at[i], out[0].at[at[slot]]))
+                slot += 1
+        return copies
+
+    return copy_call(
+        copies_of,
+        near_at + far_at,
+        operands,
+        [jax.ShapeDtypeStruct((fsdp_size,) + near[0].shape[-2:], near[0].dtype)],
+        fsdp_size,
+        (pltpu.VMEM, pl.ANY),
+    )[0]
+
+
+def split_rows(grads, extra=None):
+    fsdp_size = lax.axis_size("fsdp")
+    columns = fsdp_size // 2
+    place = lax.axis_index("fsdp")
+    column, side = place // 2, place % 2
+    parts = [grads] if extra is None else [grads, extra]
+    rows = [part.shape[1] for part in parts]
+    firsts = [0, rows[0]]
+    order = [(column + step) % columns for step in range(columns)]
+
+    def copies_of(at, own, out):
+        copies = []
+        for part, first, count in zip(own, firsts, rows):
+            span = pl.ds(first, count)
+            for i in range(columns):
+                copies.append((part.at[at[i]], out[0].at[i, span]))
+                copies.append((part.at[at[columns + i]], out[1].at[i, span]))
+        return copies
+
+    shape = jax.ShapeDtypeStruct((columns, sum(rows), grads.shape[-1]), jnp.bfloat16)
+    return copy_call(
+        copies_of,
+        [c * 2 + side for c in order] + [c * 2 + 1 - side for c in order],
+        parts,
+        [shape, shape],
+        2 * columns * len(parts),
+        (pl.ANY, pltpu.VMEM),
+    )
+
+
+def wide_sum(*values):
+    total = values[0].astype(jnp.float32)
+    for value in values[1:]:
+        total = total + value.astype(jnp.float32)
+    return total
+
+
+def turn_sums(stay, got):
+    columns, _, turn = ring_pairs(lax.axis_size("fsdp"))
+    return [
+        lax.ppermute(
+            wide_sum(stay[step], got[step]).astype(jnp.bfloat16), "fsdp", turn(step)
+        )
+        for step in range(1, columns)
+    ]
+
+
+def head_prep(raw, gain, cosine, sine):
+    recip = lax.rsqrt(jnp.mean(raw * raw, axis=-1, keepdims=True) + EPS)
+    hat = raw * recip
+    scaled = hat * gain
+    half_size = raw.shape[-1] // 2
+    return hat, recip, scaled * cosine + pltpu.roll(scaled, half_size, 1) * sine
+
+
+def head_back(grad, gain, cosine, sine, hat, recip):
+    half_size = grad.shape[-1] // 2
+    unrot = grad * cosine - pltpu.roll(grad, half_size, 1) * sine
+    gain_grad = jnp.sum(unrot * hat, axis=0, keepdims=True)
+    scaled = unrot * gain
+    return gain_grad, recip * (scaled - hat * jnp.mean(scaled * hat, axis=-1, keepdims=True))
+
+
+def nt_dot(left, right):
+    return lax.dot_general(
+        left, right, (((1,), (1,)), ((), ())), preferred_element_type=jnp.float32
+    )
+
+
+LOG2_E = 1.4426950408889634
+
+
+def key_mask(segment_col, segment_row, key_rows, query_rows, diagonal):
+    same = segment_col[key_rows, :] == segment_row[:, query_rows]
+    if not diagonal:
+        return same
+    size = (key_rows.stop - key_rows.start, query_rows.stop - query_rows.start)
+    key_at = lax.broadcasted_iota(jnp.int32, size, 0)
+    query_at = lax.broadcasted_iota(jnp.int32, size, 1)
+    return same & (key_at <= query_at)
+
+
+def attend_kernel(
+    group_size,
+    block,
+    raw_ref,
+    cosine_ref,
+    sine_ref,
+    qgain_ref,
+    kgain_ref,
+    segment_col,
+    segment_row,
+    out_ref,
+    lse_ref,
+    query_scr,
+    key_scr,
+    value_scr,
+):
+    tok_count, head_size = cosine_ref.shape
+    factor = head_size ** (-0.5) * LOG2_E
+    blocks = [slice(i, i + block) for i in range(0, tok_count, block)]
+    key_col, value_col = group_size * head_size, (group_size + 1) * head_size
+    for rows in blocks:
+        cosine, sine = cosine_ref[rows, :], sine_ref[rows, :]
+        for h in range(group_size):
+            cols = slice(h * head_size, (h + 1) * head_size)
+            query_scr[rows, cols] = head_prep(raw_ref[rows, cols], qgain_ref[...], cosine, sine)[
+                2
+            ].astype(jnp.bfloat16)
+        key_scr[rows, :] = head_prep(
+            raw_ref[rows, key_col:value_col], kgain_ref[...], cosine, sine
+        )[2].astype(jnp.bfloat16)
+        value_scr[:, rows] = raw_ref[rows, value_col:].T.astype(jnp.bfloat16)
+    for h in range(group_size):
+        cols = slice(h * head_size, (h + 1) * head_size)
+        for i, query_rows in enumerate(blocks):
+            query = query_scr[query_rows, cols]
+            total = jnp.zeros((1, block), jnp.float32)
+            mixed = jnp.zeros((head_size, block), jnp.float32)
+            for j, key_rows in enumerate(blocks[: i + 1]):
+                scores = nt_dot(key_scr[key_rows, :], query)
+                mask = key_mask(segment_col, segment_row, key_rows, query_rows, i == j)
+                terms = jnp.where(mask, jnp.exp2(scores * factor), 0.0)
+                total = total + jnp.sum(terms, axis=0, keepdims=True)
+                mixed = mixed + jnp.dot(
+                    value_scr[:, key_rows],
+                    terms.astype(jnp.bfloat16),
+                    preferred_element_type=jnp.float32,
+                )
+            out_ref[query_rows, cols] = (mixed * (1.0 / total)).T.astype(jnp.bfloat16)
+            lse_ref[0, h : h + 1, query_rows] = jnp.log2(total)
+
+
+def attend_back_kernel(
+    group_size,
+    block,
+    raw_ref,
+    out_ref,
+    grad_ref,
+    lse_ref,
+    cosine_ref,
+    sine_ref,
+    qgain_ref,
+    kgain_ref,
+    segment_col,
+    segment_row,
+    back_ref,
+    gains_ref,
+    hat_scr,
+    recip_scr,
+    query_scr,
+    key_scr,
+    key_turned,
+    value_scr,
+    grad_key,
+    grad_value,
+):
+    tok_count, head_size = cosine_ref.shape
+    scale = head_size ** (-0.5)
+    factor = scale * LOG2_E
+    blocks = [slice(i, i + block) for i in range(0, tok_count, block)]
+    key_col, value_col = group_size * head_size, (group_size + 1) * head_size
+    head_cols = [slice(h * head_size, (h + 1) * head_size) for h in range(group_size + 1)]
+    for rows in blocks:
+        cosine, sine = cosine_ref[rows, :], sine_ref[rows, :]
+        for h, cols in enumerate(head_cols):
+            gain = qgain_ref[...] if h < group_size else kgain_ref[...]
+            hat, recip, turned = head_prep(raw_ref[rows, cols], gain, cosine, sine)
+            hat_scr[rows, cols] = hat
+            recip_scr[rows, cols] = jnp.broadcast_to(recip, hat.shape)
+            if h < group_size:
+                query_scr[rows, cols] = turned.astype(jnp.bfloat16)
+            else:
+                key_scr[rows, :] = turned.astype(jnp.bfloat16)
+                key_turned[:, rows] = turned.T.astype(jnp.bfloat16)
+        value_scr[rows, :] = raw_ref[rows, value_col:].astype(jnp.bfloat16)
+    query_gain_grad = jnp.zeros((1, head_size), jnp.float32)
+    for h, cols in enumerate(head_cols[:group_size]):
+        for i, query_rows in enumerate(blocks):
+            query = query_scr[query_rows, cols]
+            grad = grad_ref[query_rows, cols]
+            delta = jnp.sum(
+                (grad.astype(jnp.float32) * out_ref[query_rows, cols].astype(jnp.float32)).T,
+                axis=0,
+                keepdims=True,
+            )
+            lse = lse_ref[0, h : h + 1, query_rows]
+            grad_query = jnp.zeros((head_size, block), jnp.float32)
+            for j, key_rows in enumerate(blocks[: i + 1]):
+                scores = nt_dot(key_scr[key_rows, :], query)
+                mask = key_mask(segment_col, segment_row, key_rows, query_rows, i == j)
+                probs = jnp.where(mask, jnp.exp2(scores * factor - lse), 0.0)
+                grad_probs = nt_dot(value_scr[key_rows, :], grad)
+                grad_scores = (probs * (grad_probs - delta)).astype(jnp.bfloat16)
+                value_part = jnp.dot(
+                    probs.astype(jnp.bfloat16), grad, preferred_element_type=jnp.float32
+                )
+                key_part = jnp.dot(grad_scores, query, preferred_element_type=jnp.float32)
+                grad_query = grad_query + jnp.dot(
+                    key_turned[:, key_rows], grad_scores, preferred_element_type=jnp.float32
+                )
+                if h == 0 and i == j:
+                    grad_value[key_rows, :] = value_part
+                    grad_key[key_rows, :] = key_part
+                else:
+                    grad_value[key_rows, :] += value_part
+                    grad_key[key_rows, :] += key_part
+            gain_grad, back = head_back(
+                grad_query.T * scale,
+                qgain_ref[...],
+                cosine_ref[query_rows, :],
+                sine_ref[query_rows, :],
+                hat_scr[query_rows, cols],
+                recip_scr[query_rows, cols],
+            )
+            query_gain_grad = query_gain_grad + gain_grad
+            back_ref[query_rows, cols] = back.astype(jnp.bfloat16)
+    key_gain_grad = jnp.zeros((1, head_size), jnp.float32)
+    for rows in blocks:
+        gain_grad, back = head_back(
+            grad_key[rows, :] * scale,
+            kgain_ref[...],
+            cosine_ref[rows, :],
+            sine_ref[rows, :],
+            hat_scr[rows, head_cols[-1]],
+            recip_scr[rows, head_cols[-1]],
+        )
+        key_gain_grad = key_gain_grad + gain_grad
+        back_ref[rows, key_col:value_col] = back.astype(jnp.bfloat16)
+        back_ref[rows, value_col:] = grad_value[rows, :].astype(jnp.bfloat16)
+    gains_ref[0, 0:1, :] = query_gain_grad
+    gains_ref[0, 1:2, :] = key_gain_grad
+
+
+def attention_calls(tok_count, head_size, group_size, kv_heads):
+    block = min(256, tok_count)
+    wide = (group_size + 2) * head_size
+    whole = pl.BlockSpec((tok_count, head_size), lambda g: (0, 0))
+    gain = pl.BlockSpec((1, head_size), lambda g: (0, 0))
+    common = [
+        whole,
+        whole,
+        gain,
+        gain,
+        pl.BlockSpec((tok_count, 1), lambda g: (0, 0)),
+        pl.BlockSpec((1, tok_count), lambda g: (0, 0)),
+    ]
+    raw = pl.BlockSpec((tok_count, wide), lambda g: (0, g))
+    heads = pl.BlockSpec((tok_count, group_size * head_size), lambda g: (0, g))
+    lse = pl.BlockSpec((1, group_size, tok_count), lambda g: (g, 0, 0))
+    pairs = kv_heads * group_size * tok_count * tok_count
+    low, full = jnp.bfloat16, jnp.float32
+    limit = pltpu.CompilerParams(vmem_limit_bytes=44 * 1024 * 1024)
+
+    def forward(earlier, *operands):
+        count = len(earlier)
+        return pl.pallas_call(
+            lambda *refs: attend_kernel(group_size, block, *refs[count:]),
+            grid=(kv_heads,),
+            in_specs=[pl.BlockSpec(memory_space=pl.ANY)] * count + [raw] + common,
+            out_specs=[heads, lse],
+            out_shape=[
+                jax.ShapeDtypeStruct((tok_count, kv_heads * group_size * head_size), low),
+                jax.ShapeDtypeStruct((kv_heads, group_size, tok_count), full),
+            ],
+            scratch_shapes=[
+                pltpu.VMEM((tok_count, group_size * head_size), low),
+                pltpu.VMEM((tok_count, head_size), low),
+                pltpu.VMEM((head_size, tok_count), low),
+            ],
+            compiler_params=limit,
+            cost_estimate=pl.CostEstimate(
+                flops=pairs, bytes_accessed=0, transcendentals=0
+            ),
+        )(*earlier, *operands)
+
+    def backward(earlier, *operands):
+        count = len(earlier)
+        return pl.pallas_call(
+            lambda *refs: attend_back_kernel(group_size, block, *refs[count:]),
+            grid=(kv_heads,),
+            in_specs=[pl.BlockSpec(memory_space=pl.ANY)] * count + [raw, heads, heads, lse] + common,
+            out_specs=[raw, pl.BlockSpec((1, 2, head_size), lambda g: (g, 0, 0))],
+            out_shape=[
+                jax.ShapeDtypeStruct((tok_count, kv_heads * wide), low),
+                jax.ShapeDtypeStruct((kv_heads, 2, head_size), full),
+            ],
+            scratch_shapes=[
+                pltpu.VMEM((tok_count, (group_size + 1) * head_size), full),
+                pltpu.VMEM((tok_count, (group_size + 1) * head_size), full),
+                pltpu.VMEM((tok_count, group_size * head_size), low),
+                pltpu.VMEM((tok_count, head_size), low),
+                pltpu.VMEM((head_size, tok_count), low),
+                pltpu.VMEM((tok_count, head_size), low),
+                pltpu.VMEM((tok_count, head_size), full),
+                pltpu.VMEM((tok_count, head_size), full),
+            ],
+            compiler_params=limit,
+            cost_estimate=pl.CostEstimate(
+                flops=pairs, bytes_accessed=0, transcendentals=0
+            ),
+        )(*earlier, *operands)
+
+    return forward, backward
+
+
+def sum_cores(partial_of, c_index):
+    got = swap(partial_of(1 - c_index).astype(jnp.bfloat16), "tensor")
+    return (partial_of(c_index) + got.astype(jnp.float32)).astype(jnp.bfloat16)
+
+
+def cross_sum(mine):
+    return wide_sum(mine, swap(mine, "context")).astype(jnp.bfloat16)
+
+
+def sum_part(mine, x_index):
+    got = swap(half_of(mine, 1 - x_index, 0), "context")
+    return wide_sum(half_of(mine, x_index, 0), got)
+
+
+def dot_rows(left, right):
+    return jnp.dot(left, right, preferred_element_type=jnp.float32)
+
+
+def dot_back(left, right):
+    return jnp.einsum("pf,df->pd", left, right, preferred_element_type=jnp.float32)
+
+
+def dot_grad(left, right):
+    return jnp.einsum("pd,pf->df", left, right, preferred_element_type=jnp.float32)
+
+
+def quarter_shards(
+    hidden_in,
+    cotangent,
+    segment,
+    position,
+    w_query,
+    w_key,
+    w_value,
+    w_output,
+    w_gate,
+    w_up,
+    w_down,
+    attn_gain,
+    ffn_gain,
+    query_gain,
+    key_gain,
+):
+    x_index, c_index = lax.axis_index("context"), lax.axis_index("tensor")
+    fsdp_size = lax.axis_size("fsdp")
+    rows_shard = w_query.shape[0]
+    model = rows_shard * fsdp_size
+    head_size = query_gain.shape[0] * fsdp_size
+    q_width, kv_width = w_query.shape[1] // 2, w_key.shape[1] // 2
+    ff_width = w_gate.shape[1] // 2
+    q_heads, kv_heads = q_width // head_size, kv_width // head_size
+    group_size = q_heads // kv_heads
+    group_width = group_size * head_size
+
+    def mine(weight, axis):
+        return half_of(weight, x_index, axis)
+
+    gains = jnp.concatenate([attn_gain, ffn_gain, query_gain, key_gain])
+    gain_rows = jnp.pad(gains[None], ((0, 15), (0, q_width + 2 * kv_width - gains.shape[0])))
+    blob_a = pack_call(x_index, kv_heads, head_size, w_query, w_key, w_value, gain_rows)
+    blob_o = mine(w_output, 0).T
+    blob_g, blob_u = mine(w_gate, 1), mine(w_up, 1)
+    blob_d = mine(w_down, 0).T
+
+    def own_part(rows):
+        return half_of(half_of(rows, x_index, 0), c_index, 1)
+
+    def wide_half(weight, h):
+        return half_of(weight, h, 0)
+
+    def grouped(grads):
+        return grads.astype(jnp.bfloat16).reshape(fsdp_size, rows_shard, -1)
+
+    def stacked(pieces):
+        return stack_pieces(pieces[0], pieces[1:])
+
+    turned_a = turn_pieces(blob_a)
+    far_own_a = flip_pieces(blob_a)
+    hidden_got = swap(hidden_in[0], "context")
+    turned_a, far_own_a, hidden_got, blob_o, blob_g, blob_u, blob_d = fence(
+        turned_a, far_own_a, hidden_got, blob_o, blob_g, blob_u, blob_d
+    )
+
+    near_a = stack_pieces(turned_a[1], turned_a[2:])
+    far_a = flip_pieces(near_a)
+    turned_o = turn_pieces(blob_o)
+    marks = jnp.stack([segment[0], position[0]])
+    marks = pair_join(x_index, marks, swap(marks, "context"), 1)
+    hidden_column = pair_join(x_index, hidden_in[0], hidden_got, 0)
+    hidden_other = swap(hidden_column, "tensor")
+    hidden_rows = pair_join(c_index, hidden_column, hidden_other, 1)
+    x_rows = hidden_rows.astype(jnp.float32)
+    tok_count = x_rows.shape[0]
+    recip_one = norm_stats(x_rows)
+    segment_all, position_all = marks[0], marks[1]
+    half_size = head_size // 2
+    freq_table = THETA ** (-jnp.arange(half_size, dtype=jnp.float32) * 2.0 / head_size)
+    angle_table = position_all.astype(jnp.float32)[:, None] * freq_table[None, :]
+    cosine_half, sine_half = jnp.cos(angle_table), jnp.sin(angle_table)
+    cosine_table = jnp.concatenate([cosine_half, cosine_half], axis=1)
+    sine_table = jnp.concatenate([-sine_half, sine_half], axis=1)
+    (
+        far_a, turned_o, hidden_rows, recip_one, cosine_table, sine_table, blob_g, turned_a,
+        far_own_a, cotangent,
+    ) = fence(
+        far_a, turned_o, hidden_rows, recip_one, cosine_table, sine_table, blob_g, turned_a,
+        far_own_a, cotangent,
+    )
+
+    near_o = stacked(turned_o)
+    far_o = flip_pieces(near_o)
+    turned_g = turn_pieces(blob_g)
+    dy_got = swap(cotangent[0], "context")
+    all_a = place_rows(turned_a, [far_own_a, far_a])
+    w_qkv = all_a[:, :rows_shard].reshape(model, -1)
+    gain_all = all_a[:, rows_shard].astype(jnp.float32)
+    gain_part = query_gain.shape[0]
+    attn_gain32 = gain_all[:, :rows_shard].reshape(model)
+    ffn_gain32 = gain_all[:, rows_shard : 2 * rows_shard].reshape(model)
+    qgain32 = gain_all[:, 2 * rows_shard : 2 * rows_shard + gain_part].reshape(head_size)
+    kgain32 = gain_all[:, 2 * rows_shard + gain_part : 2 * rows_shard + 2 * gain_part].reshape(
+        head_size
+    )
+    x_rows = hidden_rows.astype(jnp.float32)
+    attn_in = (x_rows * recip_one * attn_gain32).astype(jnp.bfloat16)
+    qkv_raw = dot_rows(attn_in, w_qkv)
+    qkv_raw, far_o, near_o, turned_g, dy_got, blob_u = fence(
+        qkv_raw, far_o, near_o, turned_g, dy_got, blob_u
+    )
+
+    near_g = stacked(turned_g)
+    far_g = flip_pieces(near_g)
+    turned_u = turn_pieces(blob_u)
+    attend, attend_back = attention_calls(tok_count, head_size, group_size, kv_heads)
+    shared = (
+        cosine_table,
+        sine_table,
+        qgain32[None],
+        kgain32[None],
+        segment_all[:, None],
+        segment_all[None, :],
+    )
+    attn_low, log_total = attend((), qkv_raw, *shared)
+    all_o = place_rows([near_o], [far_o]).reshape(model, -1)
+    attn_low, all_o, far_g, near_g, turned_u, blob_d, dy_got, cotangent = fence(
+        attn_low, all_o, far_g, near_g, turned_u, blob_d, dy_got, cotangent
+    )
+
+    near_u = stacked(turned_u)
+    far_u = flip_pieces(near_u)
+    turned_d = turn_pieces(blob_d)
+    attn_mine = sum_cores(lambda h: dot_back(attn_low, wide_half(all_o, h)), c_index)
+    attn_total = cross_sum(attn_mine)
+    all_g = place_rows([near_g], [far_g]).reshape(model, -1)
+    dy_column = pair_join(x_index, cotangent[0], dy_got, 0)
+    rows_dy = pair_join(c_index, dy_column, swap(dy_column, "tensor"), 1)
+    attn_total, all_g, far_u, near_u, turned_d, rows_dy = fence(
+        attn_total, all_g, far_u, near_u, turned_d, rows_dy
+    )
+
+    attn_other = swap(attn_total, "tensor")
+    near_d = stacked(turned_d)
+    far_d = flip_pieces(near_d)
+    all_u = place_rows([near_u], [far_u]).reshape(model, -1)
+    mid_rows = x_rows + pair_join(c_index, attn_total, attn_other, 1).astype(jnp.float32)
+    recip_two = norm_stats(mid_rows)
+    normed_two = mid_rows * recip_two
+    ffn_in = (normed_two * ffn_gain32).astype(jnp.bfloat16)
+    gate_pre, up_pre = dot_rows(ffn_in, all_g), dot_rows(ffn_in, all_u)
+    gate_sig = jax.nn.sigmoid(gate_pre)
+    hidden_low = (gate_pre * gate_sig * up_pre).astype(jnp.bfloat16)
+    stay_d, away_d = split_rows(grouped(dot_grad(rows_dy, hidden_low)))
+    gate_pre, up_pre, far_d, near_d, ffn_in, all_g, all_u, stay_d, away_d, hidden_low = fence(
+        gate_pre, up_pre, far_d, near_d, ffn_in, all_g, all_u, stay_d, away_d, hidden_low
+    )
+
+    got_d = flip_pieces(away_d)
+    gate_sig = jax.nn.sigmoid(gate_pre)
+    gate_act = gate_pre * gate_sig
+    all_d = place_rows([near_d], [far_d]).reshape(model, -1)
+    grad_hidden = dot_rows(rows_dy, all_d)
+    grad_gate = (grad_hidden * up_pre * gate_sig * (1.0 + gate_pre * (1.0 - gate_sig))).astype(
+        jnp.bfloat16
+    )
+    grad_up_pre = (grad_hidden * gate_act).astype(jnp.bfloat16)
+    ffn_mine = sum_cores(
+        lambda h: dot_back(grad_gate, wide_half(all_g, h))
+        + dot_back(grad_up_pre, wide_half(all_u, h)),
+        c_index,
+    )
+    sent_d = turn_sums(after(stay_d, ffn_mine), got_d)
+    stay_g, away_g = split_rows(grouped(dot_grad(ffn_in, after(grad_gate, ffn_mine))))
+    got_g = flip_pieces(after(away_g, got_d))
+    stay_u, away_u = split_rows(grouped(dot_grad(ffn_in, after(grad_up_pre, ffn_mine))))
+    ffn_total = cross_sum(ffn_mine)
+    (
+        ffn_total, stay_d, got_d, sent_d, stay_g, got_g, stay_u, away_u, hidden_low, rows_dy,
+        mid_rows, all_d,
+    ) = fence(
+        ffn_total, stay_d, got_d, sent_d, stay_g, got_g, stay_u, away_u, hidden_low, rows_dy,
+        mid_rows, all_d,
+    )
+
+    def finish(stay, got, sent):
+        low = wide_sum(stay[0], got[0], *sent).astype(jnp.bfloat16)
+        return low, swap(low, "context")
+
+    ffn_other = swap(ffn_total, "tensor")
+    sent_g = turn_sums(stay_g, got_g)
+    got_u = flip_pieces(away_u)
+    grad_ffn_in = pair_join(c_index, ffn_total, ffn_other, 1).astype(jnp.float32)
+    normed_two = mid_rows * recip_two
+    grad_ffn_gain = jnp.sum(grad_ffn_in * normed_two, axis=0)
+    grad_mid = rows_dy.astype(jnp.float32) + norm_back(
+        grad_ffn_in * ffn_gain32, normed_two, recip_two
+    )
+    grad_mid_low = grad_mid.astype(jnp.bfloat16)
+    grad_attn = dot_rows(grad_mid_low, all_o).astype(jnp.bfloat16)
+    stay_o, away_o = split_rows(grouped(dot_grad(grad_mid_low, attn_low)))
+    grad_qkv, head_gains = attend_back((away_o,), qkv_raw, attn_low, grad_attn, log_total, *shared)
+    got_o = flip_pieces(after(away_o, got_u))
+    own_d, far_d = finish(stay_d, got_d, sent_d)
+    (
+        sent_g, got_u, grad_qkv, head_gains, got_o, stay_o, stay_u, stay_g, got_g, attn_in,
+        hidden_low, mid_rows, all_d,
+    ) = fence(
+        sent_g, got_u, grad_qkv, head_gains, got_o, stay_o, stay_u, stay_g, got_g, attn_in,
+        hidden_low, mid_rows, all_d,
+    )
+
+    sent_u = turn_sums(stay_u, got_u)
+    normed_one = x_rows * recip_one
+    gain_halves = {}
+
+    def attn_part(h):
+        part = dot_back(grad_qkv, wide_half(w_qkv, h))
+        gain_halves[len(gain_halves)] = jnp.sum(part * half_of(normed_one, h, 1), axis=0)
+        return part
+
+    attn_in_mine = sum_cores(attn_part, c_index)
+    grad_attn_gain = pair_join(c_index, gain_halves[1], gain_halves[0], 0)
+    head_gains = jnp.sum(head_gains, axis=0)
+    first_device = (x_index == 0) & (c_index == 0)
+    gain_block = jnp.concatenate(
+        [
+            grad_attn_gain.reshape(fsdp_size, rows_shard),
+            jnp.where(first_device, grad_ffn_gain, 0.0).reshape(fsdp_size, rows_shard),
+            head_gains[0].reshape(fsdp_size, gain_part),
+            head_gains[1].reshape(fsdp_size, gain_part),
+        ],
+        axis=1,
+    ).astype(jnp.bfloat16)
+    gain_block = gain_block.astype(jnp.float32) + swap(gain_block, "tensor").astype(jnp.float32)
+    gain_block = jnp.pad(
+        gain_block.astype(jnp.bfloat16)[:, None],
+        ((0, 0), (0, 15), (0, grad_qkv.shape[1] - gain_block.shape[1])),
+    )
+    stay_a, away_a = split_rows(grouped(dot_grad(attn_in, grad_qkv)), gain_block)
+    got_a = flip_pieces(away_a)
+    sent_o = turn_sums(after(stay_o, *sent_u), got_o)
+    own_g, far_g = finish(stay_g, got_g, sent_g)
+    attn_in_part = sum_part(attn_in_mine, x_index).astype(jnp.bfloat16)
+    (
+        sent_u, got_a, sent_o, attn_in_part, stay_a, stay_o, got_o, stay_u, got_u, hidden_low,
+        mid_rows, all_d,
+    ) = fence(
+        sent_u, got_a, sent_o, attn_in_part, stay_a, stay_o, got_o, stay_u, got_u, hidden_low,
+        mid_rows, all_d,
+    )
+
+    sent_a = turn_sums(stay_a, got_a)
+    out_mine = sum_cores(lambda h: dot_back(hidden_low, wide_half(all_d, h)), c_index)
+    block_out = (own_part(mid_rows) + sum_part(out_mine, x_index)).astype(jnp.bfloat16)[None]
+    own_u, far_u = finish(stay_u, got_u, sent_u)
+    own_o, far_o = finish(stay_o, got_o, sent_o)
+    grad_attn_in = pair_join(c_index, attn_in_part, swap(attn_in_part, "tensor"), 1).astype(
+        jnp.float32
+    )
+    normed_part = half_of(x_rows * recip_one, x_index, 0)
+    grad_input = half_of(grad_mid, x_index, 0) + norm_back(
+        grad_attn_in * attn_gain32, normed_part, half_of(recip_one, x_index, 0)
+    )
+    grad_input_part = half_of(grad_input, c_index, 1)[None]
+    own_a, far_a = finish(stay_a, got_a, sent_a)
+    gain_sum = own_a[rows_shard].astype(jnp.float32) + far_a[rows_shard].astype(jnp.float32)
+
+    def outcome(own, far):
+        return pair_join(x_index, own, far, 1).astype(jnp.float32)
+
+    def outcome_columns(own, far):
+        return pair_join(x_index, own.T, far.T, 0).astype(jnp.float32)
+
+    def picked(first, size):
+        wide = group_width + 2 * head_size
+        starts = [g * wide + first for g in range(kv_heads)]
+        own = jnp.concatenate([own_a[:rows_shard, s : s + size] for s in starts], axis=1)
+        far = jnp.concatenate([far_a[:rows_shard, s : s + size] for s in starts], axis=1)
+        return pair_join(x_index, own, far, 1).astype(jnp.float32)
+
+    return (
+        block_out,
+        grad_input_part,
+        picked(0, group_width),
+        picked(group_width, head_size),
+        picked(group_width + head_size, head_size),
+        outcome_columns(own_o, far_o),
+        outcome(own_g, far_g),
+        outcome(own_u, far_u),
+        outcome_columns(own_d, far_d),
+        gain_sum[:rows_shard],
+        gain_sum[rows_shard : 2 * rows_shard],
+        gain_sum[2 * rows_shard : 2 * rows_shard + gain_part],
+        gain_sum[2 * rows_shard + gain_part : 2 * rows_shard + 2 * gain_part],
+    )
+
+
+def fits_quarters(mesh):
+    sizes = mesh.shape
+    return sizes["context"] == 2 and sizes["tensor"] == 2 and sizes["fsdp"] % 2 == 0
+
+
 def solution(mesh):
     in_specs = (
         P("fsdp", "context", "tensor"),
@@ -378,4 +1153,5 @@
         P("fsdp"),
         P("fsdp"),
     )
+    shards = quarter_shards if fits_quarters(mesh) else plain_shards
     return jax.shard_map(shards, mesh=mesh, in_specs=in_specs, out_specs=out_specs, check_vma=False)

time: 1230 us -> 385 us (0.31)
  waiting for transfers between devices: 867 us -> 141 us
  blocking collectives: 91.7 us -> 0 us
  matrix products: 128 us -> 39.4 us
  starting transfers between devices: 1.43 us -> 65.3 us
  Pallas kernels: 0 us -> 53.3 us
  local copies, waits for them, and re-layouts: 46 us -> 25.2 us
  other arithmetic: 69.3 us -> 51.9 us
  between operations: 17.5 us -> 2.4 us
    reduce_scatter x7 -> x0, waiting for transfers between devices: 356 us -> none  [the longest x1 77.7 us: shards(): lax.psum_scatter(grad_w_gate.astype(jnp.bfloat16), 'fsdp', scatter_dimens...]
    all_gather x11 -> x0, waiting for transfers between devices: 332 us -> none  [the longest x1 66.4 us: shards(): lax.all_gather(w_down, 'fsdp', axis=1, tiled=True)]
    ppermute x0 -> x63, waiting for transfers between devices: none -> 141 us  [the longest x15 46 us: turn_sums(): lax.ppermute(wide_sum(stay[step], got[step]).astype(jnp.bfloat16), 'fsdp'...]
    unnamed x26 -> x0, waiting for transfers between devices: 104 us -> none
    dot_general x27 -> x20, matrix products: 128 us -> 39.4 us  [the longest x10 17.2 us: dot_back(): jnp.einsum('pf,df->pd', left, right, preferred_element_type=jnp.float32)]
    psum x4 -> x0, waiting for transfers between devices: 75.1 us -> none  [the longest x1 37.4 us: shards(): lax.psum(owned[0].astype(jnp.bfloat16), 'context').astype(jnp.float32)]
    ppermute x0 -> x63, starting transfers between devices: none -> 65.3 us  [the longest x15 20.5 us: turn_pieces(): lax.ppermute(blob, 'fsdp', turn(step))]
    pallas_call x0 -> x18, Pallas kernels: none -> 53.3 us  [the longest x15 27.9 us: copy_call(): pl.pallas_call(kernel, out_shape=shapes, in_specs=[pl.BlockSpec(memory_sp...]
  transfers between devices with their start and end apart: 24 -> 63, of which waited for: 20 -> 23; matrix products, arithmetic and copies ran while one was open for 12% -> 22% of each run, Pallas kernels for 0% -> 13%
where the time goes in v1:
time: 385 us; the launch traced here: 378 us
  waiting for transfers between devices  141 us (37%)
  starting transfers between devices  65.3 us (17%)
  Pallas kernels  53.3 us (14%)
  other arithmetic  51.9 us (13%)
  matrix products  39.4 us (10%)
  local copies, waits for them, and re-layouts  25.2 us (7%)
    ppermute x15, waiting for transfers between devices, turn_sums(): lax.ppermute(wide_sum(stay[step], got[step]).astype(jnp.bfloat16), 'fsdp'...  46 us
    ppermute x22, waiting for transfers between devices, swap(): return lax.ppermute(values, axis_name, [(0, 1), (1, 0)])  33.7 us
    ppermute x15, waiting for transfers between devices, turn_pieces(): lax.ppermute(blob, 'fsdp', turn(step))  33.6 us
    pallas_call x15, Pallas kernels, copy_call(): pl.pallas_call(kernel, out_shape=shapes, in_specs=[pl.BlockSpec(memory_sp...  27.9 us
    ppermute x11, waiting for transfers between devices, flip_pieces(): return lax.ppermute(values, 'fsdp', ring_pairs(lax.axis_size('fsdp'))[1])  27.3 us
    ppermute x15, starting transfers between devices, turn_pieces(): lax.ppermute(blob, 'fsdp', turn(step))  20.5 us
    unnamed x195, local copies, waits for them, and re-layouts  19.7 us
    ppermute x15, starting transfers between devices, turn_sums(): lax.ppermute(wide_sum(stay[step], got[step]).astype(jnp.bfloat16), 'fsdp'...  18.8 us
  transfers between devices with their start and end apart: 63, of which 23 were waited for; matrix products, arithmetic and copies ran while one was open for 22% of the time, Pallas kernels for 13%

profile of v1, /device:TPU:0, one launch (start us, length us, event | category | flops | bytes accessed | tf_op | source)
XLA Modules:
  0.0 378.1 jit_solution(5668595138448152462)
XLA Ops:
  0.7 3.0 collective-permute-start.4
  8.4 3.6 collective-permute-start.2
  16.0 3.8 %collective-permute-done.2.refs_2_.refs_3_ = bf16[144,1024]{1,0:T(8,128)(2,1)S(1)} collective-permute-done((bf16[144,1024]{1,0:T(8,128)(2,1)}, bf16[144,1024]{1,0:T(8,128)(2,1)S(1)}, u32[]{:S(2)}, u32[]{:S(2)}) %collective-permute-start.2) | collective-permute-done | bytes 294944 | tf_op jit(solution)/shard_map/ppermute | solution.py:444
  19.8 16.9 %collective-permute-done.1.refs_1_.refs_2_ = bf16[144,1024]{1,0:T(8,128)(2,1)S(1)} collective-permute-done((bf16[144,1024]{1,0:T(8,128)(2,1)}, bf16[144,1024]{1,0:T(8,128)(2,1)S(1)}, u32[]{:S(2)}, u32[]{:S(2)}) %collective-permute-start.1) | collective-permute-done | bytes 294944 | tf_op jit(solution)/shard_map/ppermute | solution.py:444
  52.9 6.6 %collective-permute-done.7.refs_2_ = bf16[128,512]{1,0:T(8,128)(2,1)S(1)} collective-permute-done((bf16[128,512]{1,0:T(8,128)(2,1)S(1)}, bf16[128,512]{1,0:T(8,128)(2,1)S(1)}, u32[]{:S(2)}, u32[]{:S(2)}) %collective-permute-start.7) | collective-permute-done | bytes 131104 | tf_op jit(solution)/shard_map/ppermute | solution.py:444
  59.5 6.1 %collective-permute-done.5.refs_5_ = bf16[3,144,1024]{2,1,0:T(8,128)(2,1)S(1)} collective-permute-done((bf16[3,144,1024]{2,1,0:T(8,128)(2,1)S(1)}, bf16[3,144,1024]{2,1,0:T(8,128)(2,1)S(1)}, u32[]{:S(2)}, u32[]{:S(2)}) %collective-permute-start.5) | collective-permute-done | bytes 884768 | tf_op jit(solution)/shard_map/ppermute | solution.py:448
  76.9 4.4 %fusion.79.refs_0_.refs_1_ = f32[1024,1024]{1,0:T(8,128)} fusion(bf16[1024,1024]{1,0:T(8,128)(2,1)S(1)} %get-tuple-element.236, bf16[1024,1024]{1,0:T(8,128)(2,1)S(1)} %bitcast.194), kind=kOutput, calls=%fused_computation.221 | convolution fusion | flops 2147483648 | bytes 8388608 | tf_op jit(solution)/shard_map/dot_general | solution.py:817
  81.3 4.6 %collective-permute-done.13.refs_2_ = bf16[128,768]{1,0:T(8,128)(2,1)S(1)} collective-permute-done((bf16[128,768]{1,0:T(8,128)(2,1)S(1)}, bf16[128,768]{1,0:T(8,128)(2,1)S(1)}, u32[]{:S(2)}, u32[]{:S(2)}) %collective-permute-start.13) | collective-permute-done | bytes 196640 | tf_op jit(solution)/shard_map/ppermute | solution.py:444
  96.9 8.0 %shard_map.250 = (bf16[1024,512]{1,0:T(8,128)(2,1)S(1)}, f32[2,2,1024]{2,1,0:T(2,128)S(1)}) custom-call(f32[1024,1024]{1,0:T(8,128)S(1)} %copy-done.2, f32[1024,128]{1,0:T(8,128)S(1)} %get-tuple-element.167.refs_1_.refs_5_, f32[1024,128]{1,0:T(8,128)S(1)} %get-tuple-element.168.refs_2_.refs_6_, f32[1,128]{1,0:T(1,128)S(1)} %broadcast_in_dim_reshape.4.refs_3_.refs_7_, ...), custom_call_target="tpu_custom_call" | custom-call | flops 4194304 | tf_op jit(solution)/shard_map/pallas_call | solution.py:752
  120.9 3.3 shard_map.253
  128.8 10.2 %collective-permute-done.21 = bf16[1024,512]{1,0:T(8,128)(2,1)S(1)} collective-permute-done((bf16[1024,512]{1,0:T(8,128)(2,1)S(1)}, bf16[1024,512]{1,0:T(8,128)(2,1)S(1)}, u32[]{:S(2)}, u32[]{:S(2)}) %collective-permute-start.21) | collective-permute-done | bytes 1048608 | tf_op jit(solution)/shard_map/ppermute | solution.py:359
  184.3 11.1 %collective-permute-done.31 = bf16[4,128,768]{2,1,0:T(8,128)(2,1)S(1)} collective-permute-done((bf16[4,128,768]{2,1,0:T(8,128)(2,1)S(1)}, bf16[4,128,768]{2,1,0:T(8,128)(2,1)S(1)}, u32[]{:S(2)}, u32[]{:S(2)}) %collective-permute-start.31) | collective-permute-done | bytes 786464 | tf_op jit(solution)/shard_map/ppermute | solution.py:448
  208.7 11.8 %collective-permute-done.33 = bf16[128,768]{1,0:T(8,128)(2,1)S(1)} collective-permute-done((bf16[128,768]{1,0:T(8,128)(2,1)S(1)}, bf16[128,768]{1,0:T(8,128)(2,1)S(1)}, u32[]{:S(2)}, u32[]{:S(2)}) %collective-permute-start.33) | collective-permute-done | bytes 196640 | tf_op jit(solution)/shard_map/ppermute | solution.py:536
  238.3 9.1 %collective-permute-done.39 = bf16[4,128,768]{2,1,0:T(8,128)(2,1)S(1)} collective-permute-done((bf16[4,128,768]{2,1,0:T(8,128)(2,1)S(1)}, bf16[4,128,768]{2,1,0:T(8,128)(2,1)S(1)}, u32[]{:S(2)}, u32[]{:S(2)}) %collective-permute-start.39) | collective-permute-done | bytes 786464 | tf_op jit(solution)/shard_map/ppermute | solution.py:448
  249.8 15.6 %shard_map.262 = (bf16[1024,1024]{1,0:T(8,128)(2,1)S(1)}, f32[2,2,128]{2,1,0:T(2,128)S(1)}) custom-call(bf16[4,128,512]{2,1,0:T(8,128)(2,1)S(1)} %get-tuple-element.229.refs_0_, f32[1024,1024]{1,0:T(8,128)} %fusion.79.refs_0_.refs_1_, bf16[1024,512]{1,0:T(8,128)(2,1)S(1)} %copy-done.13, bf16[1024,512]{1,0:T(8,128)(2,1)S(1)} %convolution_convert_fusion.5.refs_3_, ...), custom_call_target="tpu_custom_call" | custom-call | flops 4194304 | tf_op jit(solution)/shard_map/pallas_call | solution.py:774
  265.5 3.0 fusion.78
  272.2 4.1 %convolution_convert_fusion = bf16[1024,1024]{1,0:T(8,128)(2,1)S(1)} fusion(bf16[1024,1024]{1,0:T(8,128)(2,1)} %copy-done.62, bf16[1024,1024]{1,0:T(8,128)(2,1)S(1)} %copy-done.4), kind=kOutput, calls=%fused_computation.32 | convolution fusion | flops 2148532224 | bytes 6291456 | tf_op jit(solution)/shard_map/pd,pf->df/dot_general | solution.py:825
  288.4 10.9 %collective-permute-done.43 = bf16[128,768]{1,0:T(8,128)(2,1)S(1)} collective-permute-done((bf16[128,768]{1,0:T(8,128)(2,1)S(1)}, bf16[128,768]{1,0:T(8,128)(2,1)S(1)}, u32[]{:S(2)}, u32[]{:S(2)}) %collective-permute-start.43) | collective-permute-done | bytes 196640 | tf_op jit(solution)/shard_map/ppermute | solution.py:536
  306.6 5.8 %collective-permute-done.51 = bf16[512,512]{1,0:T(8,128)(2,1)S(1)} collective-permute-done((bf16[512,512]{1,0:T(8,128)(2,1)S(1)}, bf16[512,512]{1,0:T(8,128)(2,1)S(1)}, u32[]{:S(2)}, u32[]{:S(2)}) %collective-permute-start.51) | collective-permute-done | bytes 524320 | tf_op jit(solution)/shard_map/ppermute | solution.py:359
  319.3 3.6 collective-permute-start.57
  330.9 4.7 %collective-permute-done.57 = bf16[144,1024]{1,0:T(8,128)(2,1)} collective-permute-done((bf16[144,1024]{1,0:T(8,128)(2,1)}, bf16[144,1024]{1,0:T(8,128)(2,1)}, u32[]{:S(2)}, u32[]{:S(2)}) %collective-permute-start.57) | collective-permute-done | bytes 294944 | tf_op jit(solution)/shard_map/ppermute | solution.py:536
  335.6 13.8 %collective-permute-done.56 = bf16[144,1024]{1,0:T(8,128)(2,1)} collective-permute-done((bf16[144,1024]{1,0:T(8,128)(2,1)}, bf16[144,1024]{1,0:T(8,128)(2,1)}, u32[]{:S(2)}, u32[]{:S(2)}) %collective-permute-start.56) | collective-permute-done | bytes 294944 | tf_op jit(solution)/shard_map/ppermute | solution.py:536
  355.9 3.7 collective-permute-done.58
  365.0 10.3 %collective-permute-done.53 = bf16[512,512]{1,0:T(8,128)(2,1)S(1)} collective-permute-done((bf16[512,512]{1,0:T(8,128)(2,1)S(1)}, bf16[512,512]{1,0:T(8,128)(2,1)S(1)}, u32[]{:S(2)}, u32[]{:S(2)}) %collective-permute-start.53) | collective-permute-done | bytes 524320 | tf_op jit(solution)/shard_map/ppermute | solution.py:359
  (428 shorter events, 197.5 us)
Async XLA Ops:
  0.7 36.1 %collective-permute-start.4 = (bf16[512,512]{1,0:T(8,128)(2,1)}, bf16[512,512]{1,0:T(8,128)(2,1)S(1)}, u32[]{:S(2)}, u32[]{:S(2)}) collective-permute-start(bf16[512,512]{1,0:T(8,128)(2,1)} %bitcast.197), channel_id=1, source_target_pairs={{0,2},{2,0},{1,3},{3,1},{4,6},{6,4},{5,7},{7,5},{8,10},{10,8},{9,1... | collective-permute-start | bytes 1572872 | tf_op jit(solution)/shard_map/ppermute | solution.py:359
  12.0 24.8 %collective-permute-start.1 = (bf16[144,1024]{1,0:T(8,128)(2,1)}, bf16[144,1024]{1,0:T(8,128)(2,1)S(1)}, u32[]{:S(2)}, u32[]{:S(2)}) collective-permute-start(bf16[144,1024]{1,0:T(8,128)(2,1)} %shard_map.246.refs_0_), channel_id=1, source_target_pairs={{0,16},{4,20},{8,24},{12,28},{16,0},{20,4},{24,8},{28,12},{1,17},{... | collective-permute-start | bytes 884744 | tf_op jit(solution)/shard_map/ppermute | solution.py:444
  12.0 24.8 %collective-permute-start = (bf16[144,1024]{1,0:T(8,128)(2,1)}, bf16[144,1024]{1,0:T(8,128)(2,1)S(1)}, u32[]{:S(2)}, u32[]{:S(2)}) collective-permute-start(bf16[144,1024]{1,0:T(8,128)(2,1)} %shard_map.246.refs_0_), channel_id=1, source_target_pairs={{0,8},{4,12},{8,16},{12,20},{16,24},{20,28},{24,0},{28,4},{1,9},{5... | collective-permute-start | bytes 884744 | tf_op jit(solution)/shard_map/ppermute | solution.py:444
  44.6 21.0 %collective-permute-start.5 = (bf16[3,144,1024]{2,1,0:T(8,128)(2,1)S(1)}, bf16[3,144,1024]{2,1,0:T(8,128)(2,1)S(1)}, u32[]{:S(2)}, u32[]{:S(2)}) collective-permute-start(bf16[3,144,1024]{2,1,0:T(8,128)(2,1)S(1)} %shard_map.247), channel_id=1, source_target_pairs={{0,4},{4,0},{8,12},{12,8},{16,20},{20,16},{24,28},{28,24},{1,5},{5... | collective-permute-start | bytes 2654216 | tf_op jit(solution)/shard_map/ppermute | solution.py:448
  67.0 18.9 %collective-permute-start.13 = (bf16[128,768]{1,0:T(8,128)(2,1)S(1)}, bf16[128,768]{1,0:T(8,128)(2,1)S(1)}, u32[]{:S(2)}, u32[]{:S(2)}) collective-permute-start(bf16[128,768]{1,0:T(8,128)(2,1)S(1)} %get-tuple-element.172.refs_0_), channel_id=1, source_target_pairs={{0,16},{4,20},{8,24},{12,28},{16,0},{20,4},{24,8},{28,12},{1,17},{... | collective-permute-start | bytes 589832 | tf_op jit(solution)/shard_map/ppermute | solution.py:444
  87.8 18.7 %collective-permute-start.16 = (bf16[4,128,768]{2,1,0:T(8,128)(2,1)S(1)}, bf16[4,128,768]{2,1,0:T(8,128)(2,1)}, u32[]{:S(2)}, u32[]{:S(2)}) collective-permute-start(bf16[4,128,768]{2,1,0:T(8,128)(2,1)S(1)} %shard_map.252.refs_0_), channel_id=1, source_target_pairs={{0,4},{4,0},{8,12},{12,8},{16,20},{20,16},{24,28},{28,24},{1,5},{5... | collective-permute-start | bytes 2359304 | tf_op jit(solution)/shard_map/ppermute | solution.py:448
  113.7 25.3 %collective-permute-start.21 = (bf16[1024,512]{1,0:T(8,128)(2,1)S(1)}, bf16[1024,512]{1,0:T(8,128)(2,1)S(1)}, u32[]{:S(2)}, u32[]{:S(2)}) collective-permute-start(bf16[1024,512]{1,0:T(8,128)(2,1)S(1)} %add_convert_fusion.6), channel_id=1, source_target_pairs={{0,2},{2,0},{1,3},{3,1},{4,6},{6,4},{5,7},{7,5},{8,10},{10,8},{9,1... | collective-permute-start | bytes 3145736 | tf_op jit(solution)/shard_map/ppermute | solution.py:359
  117.4 24.9 %collective-permute-start.22 = (bf16[4,128,768]{2,1,0:T(8,128)(2,1)S(1)}, bf16[4,128,768]{2,1,0:T(8,128)(2,1)S(1)}, u32[]{:S(2)}, u32[]{:S(2)}) collective-permute-start(bf16[4,128,768]{2,1,0:T(8,128)(2,1)S(1)} %shard_map.254.refs_0_), channel_id=1, source_target_pairs={{0,4},{4,0},{8,12},{12,8},{16,20},{20,16},{24,28},{28,24},{1,5},{5... | collective-permute-start | bytes 2359304 | tf_op jit(solution)/shard_map/ppermute | solution.py:448
  118.9 21.3 %collective-permute-start.25 = (bf16[128,768]{1,0:T(8,128)(2,1)S(1)}, bf16[128,768]{1,0:T(8,128)(2,1)S(1)}, u32[]{:S(2)}, u32[]{:S(2)}) collective-permute-start(bf16[128,768]{1,0:T(8,128)(2,1)S(1)} %bitcast.185), channel_id=1, source_target_pairs={{0,24},{4,28},{8,0},{12,4},{16,8},{20,12},{24,16},{28,20},{1,25},{... | collective-permute-start | bytes 589832 | tf_op jit(solution)/shard_map/ppermute | solution.py:444
  119.8 21.1 %collective-permute-start.24 = (bf16[128,768]{1,0:T(8,128)(2,1)S(1)}, bf16[128,768]{1,0:T(8,128)(2,1)S(1)}, u32[]{:S(2)}, u32[]{:S(2)}) collective-permute-start(bf16[128,768]{1,0:T(8,128)(2,1)S(1)} %bitcast.186), channel_id=1, source_target_pairs={{0,16},{4,20},{8,24},{12,28},{16,0},{20,4},{24,8},{28,12},{1,17},{... | collective-permute-start | bytes 589832 | tf_op jit(solution)/shard_map/ppermute | solution.py:444
  147.0 20.0 %collective-permute-start.28 = (bf16[4,128,768]{2,1,0:T(8,128)(2,1)S(1)}, bf16[4,128,768]{2,1,0:T(8,128)(2,1)S(1)}, u32[]{:S(2)}, u32[]{:S(2)}) collective-permute-start(bf16[4,128,768]{2,1,0:T(8,128)(2,1)S(1)} %shard_map.256.refs_0_), channel_id=1, source_target_pairs={{0,4},{4,0},{8,12},{12,8},{16,20},{20,16},{24,28},{28,24},{1,5},{5... | collective-permute-start | bytes 2359304 | tf_op jit(solution)/shard_map/ppermute | solution.py:448
  175.5 20.0 %collective-permute-start.31 = (bf16[4,128,768]{2,1,0:T(8,128)(2,1)S(1)}, bf16[4,128,768]{2,1,0:T(8,128)(2,1)S(1)}, u32[]{:S(2)}, u32[]{:S(2)}) collective-permute-start(bf16[4,128,768]{2,1,0:T(8,128)(2,1)S(1)} %get-tuple-element.208), channel_id=1, source_target_pairs={{0,4},{4,0},{8,12},{12,8},{16,20},{20,16},{24,28},{28,24},{1,5},{5... | collective-permute-start | bytes 2359304 | tf_op jit(solution)/shard_map/ppermute | solution.py:448
  179.1 25.8 %collective-permute-start.30 = (bf16[1024,512]{1,0:T(8,128)(2,1)S(1)}, bf16[1024,512]{1,0:T(8,128)(2,1)S(1)}, u32[]{:S(2)}, u32[]{:S(2)}) collective-permute-start(bf16[1024,512]{1,0:T(8,128)(2,1)S(1)} %add_convert_fusion.3), channel_id=1, source_target_pairs={{0,2},{2,0},{1,3},{3,1},{4,6},{6,4},{5,7},{7,5},{8,10},{10,8},{9,1... | collective-permute-start | bytes 3145736 | tf_op jit(solution)/shard_map/ppermute | solution.py:359
  195.4 25.1 %collective-permute-start.35 = (bf16[4,128,768]{2,1,0:T(8,128)(2,1)S(1)}, bf16[4,128,768]{2,1,0:T(8,128)(2,1)S(1)}, u32[]{:S(2)}, u32[]{:S(2)}) collective-permute-start(bf16[4,128,768]{2,1,0:T(8,128)(2,1)S(1)} %get-tuple-element.214), channel_id=1, source_target_pairs={{0,4},{4,0},{8,12},{12,8},{16,20},{20,16},{24,28},{28,24},{1,5},{5... | collective-permute-start | bytes 2359304 | tf_op jit(solution)/shard_map/ppermute | solution.py:448
  222.6 25.8 %collective-permute-start.62 = (bf16[128,768]{1,0:T(8,128)(2,1)S(1)}, bf16[128,768]{1,0:T(8,128)(2,1)S(1)}, u32[]{:S(2)}, u32[]{:S(2)}) collective-permute-start(bf16[128,768]{1,0:T(8,128)(2,1)S(1)} %fusion.30), channel_id=1, source_target_pairs={{0,2},{2,0},{1,3},{3,1},{4,6},{6,4},{5,7},{7,5},{8,10},{10,8},{9,1... | collective-permute-start | bytes 589832 | tf_op jit(solution)/shard_map/ppermute | solution.py:359
  224.7 40.7 %collective-permute-start.38 = (bf16[128,768]{1,0:T(8,128)(2,1)S(1)}, bf16[128,768]{1,0:T(8,128)(2,1)S(1)}, u32[]{:S(2)}, u32[]{:S(2)}) collective-permute-start(bf16[128,768]{1,0:T(8,128)(2,1)S(1)} %get-tuple-element.326), channel_id=1, source_target_pairs={{0,24},{4,28},{8,0},{12,4},{16,8},{20,12},{24,16},{28,20},{1,25},{... | collective-permute-start | bytes 589832 | tf_op jit(solution)/shard_map/ppermute | solution.py:536
  224.8 40.7 %collective-permute-start.37 = (bf16[128,768]{1,0:T(8,128)(2,1)S(1)}, bf16[128,768]{1,0:T(8,128)(2,1)S(1)}, u32[]{:S(2)}, u32[]{:S(2)}) collective-permute-start(bf16[128,768]{1,0:T(8,128)(2,1)S(1)} %get-tuple-element.327), channel_id=1, source_target_pairs={{0,16},{4,20},{8,24},{12,28},{16,0},{20,4},{24,8},{28,12},{1,17},{... | collective-permute-start | bytes 589832 | tf_op jit(solution)/shard_map/ppermute | solution.py:536
  226.6 38.8 %collective-permute-start.36 = (bf16[128,768]{1,0:T(8,128)(2,1)S(1)}, bf16[128,768]{1,0:T(8,128)(2,1)S(1)}, u32[]{:S(2)}, u32[]{:S(2)}) collective-permute-start(bf16[128,768]{1,0:T(8,128)(2,1)S(1)} %get-tuple-element.328), channel_id=1, source_target_pairs={{0,8},{4,12},{8,16},{12,20},{16,24},{20,28},{24,0},{28,4},{1,9},{5... | collective-permute-start | bytes 589832 | tf_op jit(solution)/shard_map/ppermute | solution.py:536
  228.6 18.8 %collective-permute-start.39 = (bf16[4,128,768]{2,1,0:T(8,128)(2,1)S(1)}, bf16[4,128,768]{2,1,0:T(8,128)(2,1)S(1)}, u32[]{:S(2)}, u32[]{:S(2)}) collective-permute-start(bf16[4,128,768]{2,1,0:T(8,128)(2,1)S(1)} %copy-done.42), channel_id=1, source_target_pairs={{0,4},{4,0},{8,12},{12,8},{16,20},{20,16},{24,28},{28,24},{1,5},{5... | collective-permute-start | bytes 2359304 | tf_op jit(solution)/shard_map/ppermute | solution.py:448
  247.4 18.1 %collective-permute-start.41 = (bf16[4,128,512]{2,1,0:T(8,128)(2,1)S(1)}, bf16[4,128,512]{2,1,0:T(8,128)(2,1)S(1)}, u32[]{:S(2)}, u32[]{:S(2)}) collective-permute-start(bf16[4,128,512]{2,1,0:T(8,128)(2,1)S(1)} %get-tuple-element.229.refs_0_), channel_id=1, source_target_pairs={{0,4},{4,0},{8,12},{12,8},{16,20},{20,16},{24,28},{28,24},{1,5},{5... | collective-permute-start | bytes 1572872 | tf_op jit(solution)/shard_map/ppermute | solution.py:448
  284.5 30.1 %collective-permute-start.46 = (bf16[4,144,1024]{2,1,0:T(8,128)(2,1)S(1)}, bf16[4,144,1024]{2,1,0:T(8,128)(2,1)S(1)}, u32[]{:S(2)}, u32[]{:S(2)}) collective-permute-start(bf16[4,144,1024]{2,1,0:T(8,128)(2,1)S(1)} %get-tuple-element.239), channel_id=1, source_target_pairs={{0,4},{4,0},{8,12},{12,8},{16,20},{20,16},{24,28},{28,24},{1,5},{5... | collective-permute-start | bytes 3538952 | tf_op jit(solution)/shard_map/ppermute | solution.py:448
  317.9 33.8 %collective-permute-start.54 = (bf16[512,512]{1,0:T(8,128)(2,1)}, bf16[512,512]{1,0:T(8,128)(2,1)}, u32[]{:S(2)}, u32[]{:S(2)}) collective-permute-start(bf16[512,512]{1,0:T(8,128)(2,1)} %add_convert_fusion.8), channel_id=1, source_target_pairs={{0,1},{1,0},{2,3},{3,2},{4,5},{5,4},{6,7},{7,6},{8,9},{9,8},{10,11... | collective-permute-start | bytes 1572872 | tf_op jit(solution)/shard_map/ppermute | solution.py:359
  324.9 24.4 %collective-permute-start.56 = (bf16[144,1024]{1,0:T(8,128)(2,1)}, bf16[144,1024]{1,0:T(8,128)(2,1)}, u32[]{:S(2)}, u32[]{:S(2)}) collective-permute-start(bf16[144,1024]{1,0:T(8,128)(2,1)} %get-tuple-element.311), channel_id=1, source_target_pairs={{0,16},{4,20},{8,24},{12,28},{16,0},{20,4},{24,8},{28,12},{1,17},{... | collective-permute-start | bytes 884744 | tf_op jit(solution)/shard_map/ppermute | solution.py:536
  328.0 33.4 %collective-permute-start.52 = (bf16[1024,512]{1,0:T(8,128)(2,1)}, bf16[1024,512]{1,0:T(8,128)(2,1)S(1)}, u32[]{:S(2)}, u32[]{:S(2)}) collective-permute-start(bf16[1024,512]{1,0:T(8,128)(2,1)} %convolution_convert_fusion.4), channel_id=1, source_target_pairs={{0,1},{1,0},{2,3},{3,2},{4,5},{5,4},{6,7},{7,6},{8,9},{9,8},{10,11... | collective-permute-start | bytes 3145736 | tf_op jit(solution)/shard_map/ppermute | solution.py:359
  (134 other events, 1297.2 us)
